TPU v7x, 256 devices: a whole 4x4x8 slice. The times are simulated.
256 devices in a mesh: seg: 4 (over y_hi, core), fsdp: 64 (over x, z, y_lo).
Axes of the slice: x: 4, y: 4 (y_hi: 2, y_lo: 2; y = y_hi * 2 + y_lo), z: 8, core: 2. Of those that a mesh axis runs over, the one named last changes fastest.
Arguments:
- hidden: bfloat16 [64, 512, 8192], P('fsdp', 'seg'), may hold values from -6 to 6
- value_states: bfloat16 [64, 512, 8192], P('fsdp', 'seg'), may hold values from -6 to 6
- w_in: bfloat16 [8192, 128], P('fsdp'), may hold values from -0.0625 to 0.0625
- w_beta: bfloat16 [8192], P('fsdp'), may hold values from -0.0625 to 0.0625
- book_ids: int32 [64, 4], P('fsdp'), may hold values from 0 to 3, as said below
Outputs:
- mixed: bfloat16 [64, 512, 8192], P('fsdp', 'seg')
Inputs may be any that keep to these rules, and one draw needn't show every extreme that they name: `book_ids`: each row starts at 0 and never falls along the segments, rising by at most one from one segment to the next; a rise marks the first segment of a new book.
All inputs are finite; a program needn't handle non-finite values.
Results may differ from a plain program's by a relative error of at most 0.0075.
Values may be sent and summed in bfloat16 or wider, within the bound.
A program may use at most 128 MiB of HBM per device.

v0:
```python
import jax
import jax.numpy as jnp
from jax import lax
from jax.sharding import PartitionSpec as P

NU = 3


def from_behind(block, axis, distance):
    devices = range(lax.axis_size(axis))
    route = [(i - distance, i) for i in devices if i - distance in devices]
    return lax.ppermute(block, axis, route)


def feature_map(values_in, order_count):
    doubled = jnp.concatenate([jax.nn.relu(values_in), jax.nn.relu(-values_in)], axis=-1)
    return jnp.concatenate(
        [doubled * jnp.roll(doubled, shift_by, axis=-1) for shift_by in range(1, order_count + 1)],
        axis=-1,
    )


def fold_rows(left_side, pieces):
    return (
        jnp.dot(left_side, pieces[0], preferred_element_type=jnp.float32),
        jnp.dot(left_side, pieces[1], preferred_element_type=jnp.float32),
    )


def per_device(hidden, value_states, w_in, w_beta, book_ids):
    highest = lax.Precision.HIGHEST
    tokens = hidden[0]
    value_seg = value_states[0]
    model_width = tokens.shape[1]
    key_width = w_in.shape[1] // 2
    seg_count = lax.axis_size("seg")
    seg_index = lax.axis_index("seg")
    projected, logits = fold_rows(
        tokens,
        (
            lax.all_gather(w_in, "fsdp", axis=0, tiled=True),
            lax.all_gather(w_beta, "fsdp", axis=0, tiled=True),
        ),
    )
    beta_gate = jax.nn.sigmoid(logits)
    phi_q = feature_map(projected[:, :key_width], NU)
    phi_k = feature_map(projected[:, key_width:], NU)
    feat_width = phi_k.shape[1]
    book_row = book_ids[0]
    current_id = lax.dynamic_index_in_dim(book_row, seg_index, 0, keepdims=False)
    earlier_id = lax.dynamic_index_in_dim(
        book_row, jnp.maximum(seg_index - 1, 0), 0, keepdims=False
    )
    continues = jnp.where(seg_index > 0, current_id == earlier_id, False).astype(jnp.float32)
    key_sum = jnp.sum(phi_k, axis=0)

    def write_block(block_in, norm_in, value_block):
        key_div = jnp.maximum(jnp.dot(phi_k, norm_in, precision=highest), 1.0)
        recalled = jnp.dot(phi_k, block_in, precision=highest)
        change = beta_gate[:, None] * value_block - (beta_gate / key_div)[:, None] * recalled
        return (block_in + jnp.dot(phi_k.T, change, precision=highest)).astype(jnp.bfloat16)

    zero_mem = jnp.zeros((feat_width, model_width), jnp.bfloat16)
    zero_norm = jnp.zeros((feat_width,), jnp.float32)
    mem_in = jnp.zeros((feat_width, model_width), jnp.float32)
    norm_in = zero_norm

    def advance(mem_now_in, norm_now_in):
        return (
            write_block(mem_now_in, norm_now_in, value_seg.astype(jnp.float32)),
            norm_now_in + key_sum,
        )

    mem_now, norm_now = lax.cond(
        seg_index == 0, lambda: advance(mem_in, norm_in), lambda: (zero_mem, zero_norm)
    )
    for handoff in range(seg_count - 1):
        mem_recv, norm_recv = (
            from_behind(mem_now, "seg", 1),
            from_behind(norm_now.astype(jnp.bfloat16), "seg", 1).astype(norm_now.dtype),
        )
        here = seg_index == handoff + 1
        mem_in = jnp.where(here, continues * mem_recv.astype(jnp.float32), mem_in)
        norm_in = jnp.where(here, continues * norm_recv, norm_in)
        if handoff + 2 < seg_count:
            mem_now, norm_now = lax.cond(
                here,
                lambda m=mem_in, n=norm_in: advance(m, n),
                lambda m=mem_now, n=norm_now: (m, n),
            )
    query_div = jnp.maximum(jnp.dot(phi_q, norm_in, precision=highest), 1.0)
    mixed = (jnp.dot(phi_q, mem_in, precision=highest) / query_div[:, None]).astype(jnp.bfloat16)
    return mixed[None]


def solution(mesh):
    return jax.shard_map(
        per_device,
        mesh=mesh,
        in_specs=(
            P("fsdp", "seg", None),
            P("fsdp", "seg", None),
            P("fsdp", None),
            P("fsdp"),
            P("fsdp", None),
        ),
        out_specs=P("fsdp", "seg", None),
        check_vma=False,
    )
```

profile of v0, /device:TPU:1, one launch (start us, length us, event | category | flops | bytes accessed | tf_op | source)
XLA Modules:
  0.0 652.0 jit_solution(14659329940042266504)
XLA Ops:
  6.5 0.0 copy-start
  6.5 0.0 all-gather.3.cloned.1.call-start
  6.5 0.7 all-gather.3.cloned.1.call-update
  7.3 132.0 %all-gather = bf16[64,1,128]{2,1,0:T(2,128)(2,1)S(1)} all-gather(bf16[1,1,128]{2,1,0:T(2,128)(2,1)} %bitcast.86), channel_id=1, replica_groups=mesh['seg'=4,'fsdp'=64] {'fsdp'}, dimensions={0}, use_global_device_ids=true | all-gather | bytes 16640 | tf_op jit(solution)/shard_map/all_gather | solution.py:42
  139.3 0.0 copy-done
  139.3 0.6 fusion.50
  140.0 129.8 %all-gather.3.cloned.1.call-done = bf16[8192,128]{1,0:T(8,128)(2,1)} async-done(((bf16[128,128]{1,0:T(8,128)(2,1)}), bf16[8192,128]{1,0:T(8,128)(2,1)}) %all-gather.3.cloned.1.call-update) | async-done | bytes 2097168 | tf_op jit(solution)/shard_map/all_gather | solution.py:41
  269.8 2.5 fusion.36
  272.4 0.1 fusion.63
  272.6 0.0 copy-start.5
  272.6 3.3 conditional.3
  272.6 3.3 broadcast_in_dim.7
  275.9 48.2 %collective-permute-start.1 = (bf16[384,8192]{0,1:T(8,128)(2,1)}, bf16[384,8192]{0,1:T(8,128)(2,1)}, u32[]{:S(2)}, u32[]{:S(2)}) collective-permute-start(bf16[384,8192]{0,1:T(8,128)(2,1)} %get-tuple-element.68), channel_id=1, source_target_pairs={{0,64},{64,128},{128,192},{1,65},{65,129},{129,193},{2,66},{66,130... | collective-permute-start | bytes 18874376 | tf_op jit(solution)/shard_map/ppermute | solution.py:12
  324.1 1.9 collective-permute-start
  326.0 0.0 copy-done.5
  326.0 0.7 constant_dynamic-slice_fusion
  328.0 64.3 %collective-permute-done = bf16[384]{0:T(512)(128)(2,1)S(1)} collective-permute-done((bf16[384]{0:T(512)(128)(2,1)S(1)}, bf16[384]{0:T(512)(128)(2,1)S(1)}, u32[]{:S(2)}, u32[]{:S(2)}) %collective-permute-start) | collective-permute-done | bytes 800 | tf_op jit(solution)/shard_map/ppermute | solution.py:12
  392.3 0.0 copy-start.4
  392.3 0.0 collective-permute-done.1
  392.3 8.7 %multiply_select_fusion.1 = f32[384,8192]{0,1:T(8,128)} fusion(bf16[384,8192]{0,1:T(8,128)(2,1)} %collective-permute-done.1, f32[]{:T(128)S(6)} %convert_element_type.63, pred[]{:T(512)S(6)} %eq.22), kind=kLoop, calls=%fused_computation.33 | loop fusion | flops 9437184 | bytes 18874372 | tf_op jit(solution)/shard_map/jit(_where)/select_n | solution.py:83
  400.9 0.0 copy-done.4
  401.0 34.6 %conditional.4 = ((bf16[384,8192]{0,1:T(8,128)(2,1)}, f32[384]{0:T(512)S(1)})) conditional(s32[]{:T(128)} %convert_element_type.65, (bf16[384,8192]{0,1:T(8,128)(2,1)}, f32[384]{0:T(512)S(1)}) %conditional.3, (f32[128]{0:T(128)S(1)}, bf16[128,8192]{1,0:T(8,128)(2,1)S(1)}, f32[128,384]{0,1:T(8,128)S(1)}, f32[384]{0:T(512)S(1)}, f32[384,8192]{0,1:T(8,128)}, ...), branch_computations={%region_4.5_spmd, %region_5.6_spmd} | conditional | flops 9674752000 | bytes 92875832 | solution.py:86
  401.4 0.2 fusion.14
  401.7 0.0 copy-start.2
  401.7 17.8 %fusion.12 = f32[128,8192]{1,0:T(8,128)S(1)} fusion(f32[128,384]{0,1:T(8,128)S(1)} %get-tuple-element.111, f32[384,8192]{0,1:T(8,128)} %get-tuple-element.49, bf16[128,8192]{1,0:T(8,128)(2,1)S(1)} %get-tuple-element.51, f32[128]{0:T(128)S(1)} %fusion.14, f32[128]{0:T(128)S(1)} %get-tuple-element.50), kind=kOutput, calls=%fused_computation.17 | convolution fusion | flops 4836032512 | bytes 19072000 | tf_op jit(solution)/shard_map/cond/branch_1_fun/dot_general | solution.py:59
  419.5 0.0 copy-done.2
  419.5 16.0 %fusion.11 = bf16[384,8192]{0,1:T(8,128)(2,1)} fusion(f32[384,8192]{0,1:T(8,128)S(1)} %copy-done.2, f32[128,8192]{1,0:T(8,128)S(1)} %fusion.12, f32[128,384]{0,1:T(8,128)S(1)} %get-tuple-element.111), kind=kOutput, calls=%fused_computation.15 | convolution fusion | flops 4838129664 | bytes 23265280 | tf_op jit(solution)/shard_map/cond/branch_1_fun/dot_general | solution.py:61
  435.5 1.9 collective-permute-start.3
  437.5 1.9 collective-permute-start.2
  439.4 66.3 %collective-permute-done.2 = bf16[384]{0:T(512)(128)(2,1)S(1)} collective-permute-done((bf16[384]{0:T(512)(128)(2,1)S(1)}, bf16[384]{0:T(512)(128)(2,1)S(1)}, u32[]{:S(2)}, u32[]{:S(2)}) %collective-permute-start.2) | collective-permute-done | bytes 800 | tf_op jit(solution)/shard_map/ppermute | solution.py:12
  505.7 0.0 collective-permute-done.3
  505.7 11.6 %multiply_select_fusion = f32[384,8192]{0,1:T(8,128)} fusion(bf16[384,8192]{0,1:T(8,128)(2,1)} %collective-permute-done.3, f32[]{:T(128)S(6)} %convert_element_type.63, pred[]{:T(512)S(6)} %eq.21, bf16[384,8192]{0,1:T(8,128)(2,1)} %collective-permute-done.1, pred[]{:T(512)S(6)} %eq.22), kind=kLoop, calls=%fused_computation.32 | loop fusion | flops 18874368 | bytes 25165830 | tf_op jit(solution)/shard_map/jit(_where)/select_n | solution.py:83
  517.2 0.2 conditional.5
  517.4 40.0 %collective-permute-start.4 = (bf16[384,8192]{0,1:T(8,128)(2,1)}, bf16[384,8192]{0,1:T(8,128)(2,1)}, u32[]{:S(2)}, u32[]{:S(2)}) collective-permute-start(bf16[384,8192]{0,1:T(8,128)(2,1)} %get-tuple-element.71), channel_id=1, source_target_pairs={{0,64},{64,128},{128,192},{1,65},{65,129},{129,193},{2,66},{66,130... | collective-permute-start | bytes 18874376 | tf_op jit(solution)/shard_map/ppermute | solution.py:12
  557.5 2.1 collective-permute-start.5
  559.7 66.0 %collective-permute-done.5 = bf16[384]{0:T(512)(128)(2,1)S(1)} collective-permute-done((bf16[384]{0:T(512)(128)(2,1)S(1)}, bf16[384]{0:T(512)(128)(2,1)S(1)}, u32[]{:S(2)}, u32[]{:S(2)}) %collective-permute-start.5) | collective-permute-done | bytes 800 | tf_op jit(solution)/shard_map/ppermute | solution.py:12
  625.7 0.2 fusion.53
  625.9 0.0 collective-permute-done.4
  625.9 0.0 copy-start.1
  625.9 19.0 %fusion.29 = bf16[1,128,8192]{2,1,0:T(8,128)(2,1)} fusion(f32[384,8192]{0,1:T(8,128)} %multiply_select_fusion, bf16[384,8192]{0,1:T(8,128)(2,1)} %collective-permute-done.4, f32[]{:T(128)S(6)} %convert_element_type.63, pred[]{:T(512)S(6)} %eq.18, f32[128]{0:T(128)S(1)} %fusion.53, f32[128,128]{0,1:T(8,128)S(1)} %get-tuple-element.125, ...), kind=kOutput, calls=%fused_computation.36 | convolution fusion | flops 4843470848 | bytes 21168644 | tf_op jit(solution)/shard_map/dot_general | solution.py:92
  644.9 0.0 copy-done.1
  (22 shorter events, 0.2 us)
Async XLA Ops:
  6.5 132.8 %copy-start = (bf16[1,128,8192]{2,1,0:T(8,128)(2,1)S(1)}, bf16[1,128,8192]{2,1,0:T(8,128)(2,1)}, u32[]{:S(2)}) copy-start(bf16[1,128,8192]{2,1,0:T(8,128)(2,1)} %param.11) | copy-start | bytes 6291460
  6.5 263.2 %all-gather.3.cloned.1.call-start = ((), (), s32[]{:S(2)}) async-start(), calls=%async_computation | async-start | bytes 2129920 | tf_op jit(solution)/shard_map/all_gather | solution.py:41
  272.6 53.4 %copy-start.5 = (s32[1,4]{1,0:T(1,128)S(1)}, s32[1,4]{1,0:T(1,128)}, u32[]{:S(2)}) copy-start(s32[1,4]{1,0:T(1,128)} %param.15) | copy-start | bytes 52
  275.9 116.4 %collective-permute-start.1 = (bf16[384,8192]{0,1:T(8,128)(2,1)}, bf16[384,8192]{0,1:T(8,128)(2,1)}, u32[]{:S(2)}, u32[]{:S(2)}) collective-permute-start(bf16[384,8192]{0,1:T(8,128)(2,1)} %get-tuple-element.68), channel_id=1, source_target_pairs={{0,64},{64,128},{128,192},{1,65},{65,129},{129,193},{2,66},{66,130... | collective-permute-start | bytes 18874376 | tf_op jit(solution)/shard_map/ppermute | solution.py:12
  324.1 68.2 %collective-permute-start = (bf16[384]{0:T(512)(128)(2,1)S(1)}, bf16[384]{0:T(512)(128)(2,1)S(1)}, u32[]{:S(2)}, u32[]{:S(2)}) collective-permute-start(bf16[384]{0:T(512)(128)(2,1)S(1)} %convert_element_type.67), channel_id=1, source_target_pairs={{0,64},{64,128},{128,192},{1,65},{65,129},{129,193},{2,66},{66,130... | collective-permute-start | bytes 2312 | tf_op jit(solution)/shard_map/ppermute | solution.py:12
  392.3 8.7 %copy-start.4 = (bf16[1,128,8192]{2,1,0:T(8,128)(2,1)S(1)}, bf16[1,128,8192]{2,1,0:T(8,128)(2,1)}, u32[]{:S(2)}) copy-start(bf16[1,128,8192]{2,1,0:T(8,128)(2,1)} %param.12) | copy-start | bytes 6291460
  401.7 17.8 %copy-start.2 = (f32[384,8192]{0,1:T(8,128)S(1)}, f32[384,8192]{0,1:T(8,128)}, u32[]{:S(2)}) copy-start(f32[384,8192]{0,1:T(8,128)} %get-tuple-element.49) | copy-start | bytes 37748740 | tf_op jit(solution)/shard_map/cond
  435.5 70.1 %collective-permute-start.3 = (bf16[384,8192]{0,1:T(8,128)(2,1)}, bf16[384,8192]{0,1:T(8,128)(2,1)}, u32[]{:S(2)}, u32[]{:S(2)}) collective-permute-start(bf16[384,8192]{0,1:T(8,128)(2,1)} %get-tuple-element.70), channel_id=1, source_target_pairs={{0,64},{64,128},{128,192},{1,65},{65,129},{129,193},{2,66},{66,130... | collective-permute-start | bytes 18874376 | tf_op jit(solution)/shard_map/ppermute | solution.py:12
  437.5 68.2 %collective-permute-start.2 = (bf16[384]{0:T(512)(128)(2,1)S(1)}, bf16[384]{0:T(512)(128)(2,1)S(1)}, u32[]{:S(2)}, u32[]{:S(2)}) collective-permute-start(bf16[384]{0:T(512)(128)(2,1)S(1)} %convert_element_type.70), channel_id=1, source_target_pairs={{0,64},{64,128},{128,192},{1,65},{65,129},{129,193},{2,66},{66,130... | collective-permute-start | bytes 2312 | tf_op jit(solution)/shard_map/ppermute | solution.py:12
  517.4 108.5 %collective-permute-start.4 = (bf16[384,8192]{0,1:T(8,128)(2,1)}, bf16[384,8192]{0,1:T(8,128)(2,1)}, u32[]{:S(2)}, u32[]{:S(2)}) collective-permute-start(bf16[384,8192]{0,1:T(8,128)(2,1)} %get-tuple-element.71), channel_id=1, source_target_pairs={{0,64},{64,128},{128,192},{1,65},{65,129},{129,193},{2,66},{66,130... | collective-permute-start | bytes 18874376 | tf_op jit(solution)/shard_map/ppermute | solution.py:12
  557.5 68.2 %collective-permute-start.5 = (bf16[384]{0:T(512)(128)(2,1)S(1)}, bf16[384]{0:T(512)(128)(2,1)S(1)}, u32[]{:S(2)}, u32[]{:S(2)}) collective-permute-start(bf16[384]{0:T(512)(128)(2,1)S(1)} %convert_element_type.74), channel_id=1, source_target_pairs={{0,64},{64,128},{128,192},{1,65},{65,129},{129,193},{2,66},{66,130... | collective-permute-start | bytes 2312 | tf_op jit(solution)/shard_map/ppermute | solution.py:12
  625.9 19.0 %copy-start.1 = (bf16[1,128,8192]{2,1,0:T(8,128)(2,1)S(1)}, bf16[1,128,8192]{2,1,0:T(8,128)(2,1)}, u32[]{:S(2)}) copy-start(bf16[1,128,8192]{2,1,0:T(8,128)(2,1)} %param.11) | copy-start | bytes 6291460
Sparse Core Ops, SparseCore 0:
  9.1 260.5 all-gather.2
where the time goes:
time: 658 us; the launch traced here: 652 us
  waiting for transfers between devices  327 us (50%)
  blocking collectives  132 us (20%)
  starting transfers between devices  96.1 us (15%)
  matrix products  56.4 us (9%)
  other arithmetic  20.5 us (3%)
  between operations  15.2 us (2%)
    ppermute x6, waiting for transfers between devices, from_behind(): return lax.ppermute(block, axis, route)  197 us
    all_gather x1, blocking collectives, per_device(): lax.all_gather(w_beta, 'fsdp', axis=0, tiled=True)  132 us
    all_gather x1, waiting for transfers between devices, per_device(): lax.all_gather(w_in, 'fsdp', axis=0, tiled=True)  130 us
    ppermute x6, starting transfers between devices, from_behind(): return lax.ppermute(block, axis, route)  96.1 us
    select_n x2, other arithmetic, per_device(): mem_in = jnp.where(here, continues * mem_recv.astype(jnp.float32), mem_in)  20.2 us
    dot_general x1, matrix products, per_device(): jnp.dot(phi_q, mem_in, precision=highest) / query_div[:, None]  19 us
    dot_general x1, matrix products, write_block(): recalled = jnp.dot(phi_k, block_in, precision=highest)  17.8 us
    dot_general x1, matrix products, write_block(): jnp.dot(phi_k.T, change, precision=highest)  16 us
  transfers between devices with their start and end apart: 7, of which 4 were waited for; matrix products, arithmetic and copies ran while one was open for 0% of the time, Pallas kernels for 0%

commit v1 on v0

v1 whole, which is shorter than its diff:
```python
import functools

import jax
import jax.numpy as jnp
from jax import lax
from jax.experimental import pallas as pl
from jax.experimental.pallas import tpu as pltpu
from jax.sharding import PartitionSpec as P

NU = 3
X, Z, YL, SEGS = 4, 8, 2, 4
CHUNK = 512
EARLY = 12
MESH = pl.DeviceIdType.MESH
HIGHEST = lax.Precision.HIGHEST
F32, BF16 = jnp.float32, jnp.bfloat16


def dot(a, b):
    return jnp.dot(a, b, precision=HIGHEST, preferred_element_type=F32)


def dot_t(a, b):
    return lax.dot_general(
        a, b, (((1,), (1,)), ((), ())), precision=HIGHEST, preferred_element_type=F32
    )


def halves(u, turned, low):
    return jnp.where(low, jnp.maximum(u, 0.0), jnp.maximum(-turned, 0.0))


def phi_of(p):
    return jnp.concatenate([p * pltpu.roll(p, j, 1) for j in range(1, NU + 1)], axis=1)


def kernel(
    hidden, values, w_in, w_beta, ids, out,
    hid, wbuf, vbuf, kown, kbuf, m_hi, m_lo, acc, lacc,
    hid_sem, y_send, y_recv, x_send, x_recv, zr_send, zr_recv, zl_send, zl_recv,
    s_send, s_recv, k_send, k_recv, v_send, v_recv, r_send, r_recv, d_send, d_recv,
):
    s, f = lax.axis_index("seg"), lax.axis_index("fsdp")
    core, yl = lax.rem(s, 2), lax.rem(f, YL)
    z = lax.rem(lax.div(f, YL), Z)
    x = lax.div(f, YL * Z)
    tokens, width = hid.shape
    chunks = width // CHUNK

    def at(x_, z_, yl_):
        return (x_ * Z + z_) * YL + yl_

    sib = (s + 1 - 2 * core, f)
    cross = (lax.rem(s + 2, SEGS), f)
    y_peer = (s, at(x, z, 1 - yl))
    x_peer = [(s, at(lax.rem(x + d, X), z, yl)) for d in range(1, X)]
    right = (s, at(x, lax.rem(z + 1, Z), yl))
    left = (s, at(x, lax.rem(z + Z - 1, Z), yl))

    def remote(src, dst, send, recv, to):
        return pltpu.make_async_remote_copy(
            src_ref=src, dst_ref=dst, send_sem=send, recv_sem=recv, device_id=to, device_id_type=MESH
        )

    barrier = pltpu.get_barrier_semaphore()
    peers = [cross, sib, y_peer, *x_peer, right, left]
    for peer in peers:
        pl.semaphore_signal(barrier, inc=1, device_id=peer, device_id_type=MESH)
    hid_copy = pltpu.make_async_copy(hidden, hid, hid_sem)
    hid_copy.start()
    for r in range(SEGS - 1):

        @pl.when(s <= r)
        def _(r=r):
            kbuf[r] = jnp.zeros(kbuf.shape[1:], F32)

    own = wbuf.at[core, z, x]
    owner = core == yl

    @pl.when(owner)
    def _():
        wbuf[core, z, x, 0:128, :] = w_in[...]
        wbuf[core, z, x, 128:144, :] = jnp.broadcast_to(w_beta[...], (16, 128))

    pl.semaphore_wait(barrier, len(peers))

    y_copy = remote(own, own, y_send, y_recv, y_peer)
    pl.when(owner)(y_copy.start)

    def columns(k):
        return pl.ds(pl.multiple_of(k * CHUNK, CHUNK), CHUNK)

    def v_copy(k, slot):
        c = columns(k)
        return remote(values.at[:, c], vbuf.at[slot, :, c], v_send.at[k], v_recv.at[k], cross)

    def v_start(lo, hi):
        @pl.when(s < 2)
        def _():
            pl.loop(lo, hi)(lambda k: v_copy(k, s).start())

    v_start(0, EARLY)

    pl.when(jnp.logical_not(owner))(y_copy.wait_recv)
    x_copies = [
        remote(own, own, x_send.at[i], x_recv.at[i], peer) for i, peer in enumerate(x_peer)
    ]
    for c in x_copies:
        c.start()
    hid_copy.wait()
    acc[...] = jnp.zeros_like(acc)
    lacc[...] = jnp.zeros_like(lacc)
    for c in x_copies:
        c.wait_recv()

    def block(d):
        return lax.rem(z + d + Z, Z)

    def to_sib(i, d):
        b = wbuf.at[core, block(d)]
        return remote(b, b, s_send.at[i], s_recv.at[i], sib)

    def project(d):
        zb = block(d)

        @pl.loop(0, YL * X)
        def _(q):
            p, xb = lax.div(q, X), lax.rem(q, X)
            lo = pl.multiple_of(at(xb, zb, p) * 128, 128)
            h = hid[:, pl.ds(lo, 128)]
            acc[...] += jnp.dot(h, wbuf[p, zb, xb, 0:128, :], preferred_element_type=F32)
            lacc[...] += h.astype(F32) * wbuf[p, zb, xb, 128:144, :][0:1].astype(F32)

    half = Z // 2

    def ring(t):
        lo, n = (0, X) if t < half else (0, X // 2)
        a = wbuf.at[core, block(1 - t), pl.ds(lo, n)]
        to_r = remote(a, a, zr_send.at[t - 1], zr_recv.at[t - 1], right)
        lo = 0 if t < half else X // 2
        b = wbuf.at[core, block(t - 1), pl.ds(lo, n)]
        to_l = remote(b, b, zl_send.at[t - 1], zl_recv.at[t - 1], left)
        return to_r, to_l

    ring_copies = []
    order = [0]
    sib_copies = [to_sib(0, 0)]
    for t in range(1, half + 1):
        step = ring(t)
        for c in step:
            c.start()
        ring_copies.extend(step)
        fresh = sib_copies[-1:] if t == 1 else sib_copies[-2:]
        for c in fresh:
            c.start()
        if t > 1:
            for i in ([0] if t == 2 else [2 * t - 5, 2 * t - 4]):
                sib_copies[i].wait_recv()
                project(order[i])
        for c in step:
            c.wait_recv()
        if t < half:
            order += [-t, t]
            sib_copies += [to_sib(2 * t - 1, -t), to_sib(2 * t, t)]
        else:
            order += [half]
            sib_copies += [to_sib(2 * t - 1, half)]
    sib_copies[-1].start()
    for i in range(2 * half - 3, 2 * half):
        sib_copies[i].wait_recv()
        project(order[i])

    low = lax.broadcasted_iota(jnp.int32, (tokens, 128), 1) < 64
    low_half = low[: tokens // 2]
    proj = acc[...]
    turned = pltpu.roll(proj, 64, 1)
    logit = dot_t(jnp.ones((8, 128), F32), lacc[...])
    kown[0:64, :] = jnp.where(low_half, turned[0:64], proj[64:128])
    kown[64:72, :] = 1.0 / (1.0 + jnp.exp(-logit))

    def k_copy(src, r, i, to):
        return remote(src, kbuf.at[r], k_send.at[i], k_recv.at[r], to)

    @pl.when(s < 2)
    def _():
        k_copy(kown, s, 0, cross).start()

    v_start(EARLY, chunks)

    @pl.when(core == 0)
    def _():
        k_copy(kown, s, 1, sib).start()

    v_sib = remote(values, vbuf.at[s], d_send, d_recv, sib)
    pl.when(core == 0)(v_sib.start)

    phi_q = phi_of(halves(proj, turned, low))

    held = lax.rem(s, 2)

    @pl.when(s >= 2)
    def _():
        k_copy(kown, held, 0, cross).wait_recv()
        k_copy(kbuf.at[held], held, 2, sib).start()
        k_copy(kown, 1 - held, 0, sib).wait_recv()

    @pl.when(s == 1)
    def _():
        k_copy(kown, 0, 0, sib).wait_recv()

    @pl.when(s == 3)
    def _():
        k_copy(kown, 2, 0, sib).wait_recv()

    @pl.when(s > 0)
    def _():
        keeps, phis, betas, gains = [], [], [], []
        norm = jnp.zeros((1, 128 * NU), F32)
        for r in range(SEGS - 1):
            two = kbuf[r, 0:64, :]
            two_turned = pltpu.roll(two, 64, 1)
            p = jnp.concatenate(
                [halves(two, two_turned, low_half), halves(two_turned, two, low_half)], axis=0
            )
            phi = phi_of(p)
            beta = kbuf[r, 64:72, :]
            div = jnp.maximum(dot_t(jnp.broadcast_to(norm, (8, 128 * NU)), phi), 1.0)
            keep = jnp.where((ids[0, r + 1] == ids[0, r]) | (s < r + 1), 1.0, 0.0).astype(F32)
            phis.append(phi)
            betas.append(beta[0:1])
            gains.append((beta / div)[0:1])
            keeps.append(keep)
            norm = keep * (norm + jnp.sum(phi, axis=0, keepdims=True))
        scale = 1.0 / jnp.maximum(jnp.sum(phi_q * norm, axis=1, keepdims=True), 1.0)
        q = phi_q
        for r in reversed(range(SEGS - 1)):
            q = keeps[r] * q
            t = dot_t(q, phis[r])
            m = t * betas[r] * scale
            hi = m.astype(BF16)
            m_hi[:, 128 * r : 128 * (r + 1)] = hi
            m_lo[:, 128 * r : 128 * (r + 1)] = (m - hi.astype(F32)).astype(BF16)
            if r:
                q = q - dot(t * gains[r], phis[r])

    def mix(k, n):
        c = columns(k)
        v = vbuf[0:n, :, c].reshape(128 * n, CHUNK)
        mixed = jnp.dot(m_hi[:, : 128 * n], v, preferred_element_type=F32)
        mixed += jnp.dot(m_lo[:, : 128 * n], v, preferred_element_type=F32)
        out[:, c] = mixed.astype(BF16)

    @pl.when(s == 0)
    def _():
        out[...] = jnp.zeros_like(out)

    @pl.when(s == 1)
    def _():
        remote(values, vbuf.at[0], d_send, d_recv, sib).wait_recv()
        pl.loop(0, chunks)(lambda k: mix(k, 1))

    def relay(k, slot):
        c = columns(k)
        b = vbuf.at[slot, :, c]
        return remote(b, b, r_send.at[k], r_recv.at[k], sib)

    @pl.when(s >= 2)
    def _():
        @pl.when(s == 3)
        def _():
            remote(values, vbuf.at[2], d_send, d_recv, sib).wait_recv()

        def take(k):
            v_copy(k, held).wait_recv()
            relay(k, held).start()

        def use(k):
            relay(k, 1 - held).wait_recv()
            pl.when(s == 2)(lambda: mix(k, 2))
            pl.when(s == 3)(lambda: mix(k, 3))

        take(0)

        @pl.loop(1, chunks)
        def _(k):
            take(k)
            use(k - 1)

        use(chunks - 1)
        pl.loop(0, chunks)(lambda k: relay(k, held).wait_send())
        k_copy(kbuf.at[held], held, 2, sib).wait_send()

    pl.when(owner)(y_copy.wait_send)
    for c in (*x_copies, *ring_copies, *sib_copies):
        c.wait_send()

    @pl.when(s < 2)
    def _():
        pl.loop(0, chunks)(lambda k: v_copy(k, s).wait_send())
        k_copy(kown, s, 0, cross).wait_send()

    @pl.when(core == 0)
    def _():
        k_copy(kown, s, 1, sib).wait_send()
        v_sib.wait_send()


def per_device(hidden, value_states, w_in, w_beta, book_ids):
    _, tokens, width = hidden.shape
    chunks = width // CHUNK
    dma = pltpu.SemaphoreType.DMA
    vmem = pl.BlockSpec(memory_space=pltpu.VMEM)
    hbm = pl.BlockSpec(memory_space=pl.ANY)
    mixed = pl.pallas_call(
        kernel,
        out_shape=jax.ShapeDtypeStruct((tokens, width), BF16),
        in_specs=[hbm, hbm, vmem, vmem, pl.BlockSpec(memory_space=pltpu.SMEM)],
        out_specs=vmem,
        scratch_shapes=[
            pltpu.VMEM((tokens, width), BF16),
            pltpu.VMEM((YL, Z, X, 144, 128), BF16),
            pltpu.VMEM((SEGS - 1, tokens, width), BF16),
            pltpu.VMEM((72, 128), F32),
            pltpu.VMEM((SEGS - 1, 72, 128), F32),
            pltpu.VMEM((tokens, 128 * (SEGS - 1)), BF16),
            pltpu.VMEM((tokens, 128 * (SEGS - 1)), BF16),
            pltpu.VMEM((tokens, 128), F32),
            pltpu.VMEM((tokens, 128), F32),
            dma, dma, dma, dma((X - 1,)), dma((X - 1,)),
            dma((Z // 2,)), dma((Z // 2,)), dma((Z // 2,)), dma((Z // 2,)),
            dma((Z,)), dma((Z,)), dma((3,)), dma((SEGS - 1,)),
            dma((chunks,)), dma((chunks,)), dma((chunks,)), dma((chunks,)), dma, dma,
        ],
        compiler_params=pltpu.CompilerParams(
            collective_id=0, has_side_effects=True, vmem_limit_bytes=32 << 20
        ),
    )(hidden[0], value_states[0], w_in, w_beta.reshape(1, 128), book_ids)
    return mixed[None]


def solution(mesh):
    return jax.shard_map(
        per_device,
        mesh=mesh,
        in_specs=(
            P("fsdp", "seg", None),
            P("fsdp", "seg", None),
            P("fsdp", None),
            P("fsdp"),
            P("fsdp", None),
        ),
        out_specs=P("fsdp", "seg", None),
        check_vma=False,
    )
```

time: 658 us -> 66.7 us (0.10)
  the two profiles are of different devices: /device:TPU:1 before, /device:TPU:17 now
where the time goes in v1:
time: 66.7 us; the launch traced here: 66.4 us
  Pallas kernels  59.8 us (90%)
  local copies, waits for them, and re-layouts  6.57 us (10%)
    pallas_call x1, Pallas kernels, per_device(): pl.pallas_call(kernel, out_shape=jax.ShapeDtypeStruct((tokens, width), BF...  59.8 us
    unnamed x11, local copies, waits for them, and re-layouts  6.57 us

profile of v1, /device:TPU:17, one launch (start us, length us, event | category | flops | bytes accessed | tf_op | source)
XLA Modules:
  0.0 66.4 jit_solution(4521261499898524402)
XLA Ops:
  0.0 0.0 copy-start
  0.0 1.6 %copy-done = bf16[1,128,8192]{2,1,0:T(8,128)(2,1)S(1)} copy-done((bf16[1,128,8192]{2,1,0:T(8,128)(2,1)S(1)}, bf16[1,128,8192]{2,1,0:T(8,128)(2,1)}, u32[]{:S(2)}) %copy-start) | copy-done | bytes 2097176
  1.6 0.0 copy-start.1
  1.6 1.6 %copy-done.1 = bf16[1,128,8192]{2,1,0:T(8,128)(2,1)S(1)} copy-done((bf16[1,128,8192]{2,1,0:T(8,128)(2,1)S(1)}, bf16[1,128,8192]{2,1,0:T(8,128)(2,1)}, u32[]{:S(2)}) %copy-start.1) | copy-done | bytes 2097176
  3.2 0.0 copy-start.2
  3.2 0.8 %copy-done.2 = bf16[128,128]{1,0:T(8,128)(2,1)S(1)} copy-done((bf16[128,128]{1,0:T(8,128)(2,1)S(1)}, bf16[128,128]{1,0:T(8,128)(2,1)}, u32[]{:S(2)}) %copy-start.2) | copy-done | bytes 32792
  3.9 0.0 copy-start.3
  3.9 0.7 copy-done.3
  4.6 0.0 copy-start.4
  4.6 0.7 copy-done.4
  5.3 59.8 %shard_map.55 = bf16[128,8192]{1,0:T(8,128)(2,1)S(1)} custom-call(bf16[128,8192]{1,0:T(8,128)(2,1)S(1)} %bitcast.5, bf16[128,8192]{1,0:T(8,128)(2,1)S(1)} %bitcast.6, bf16[128,128]{1,0:T(8,128)(2,1)S(1)} %copy-done.2, bf16[1,128]{1,0:T(2,128)(2,1)S(1)} %bitcast.7, s32[1,4]{1,0:T(1,128)S(1)} %copy-done.4), custom_call_target="tpu_custom_call" | custom-call | tf_op jit(solution)/shard_map/pallas_call | solution.py:314
  65.0 1.3 %copy.7 = bf16[1,128,8192]{2,1,0:T(8,128)(2,1)} copy(bf16[1,128,8192]{2,1,0:T(8,128)(2,1)S(1)} %bitcast.4) | data formatting | bytes 4194304
Async XLA Ops:
  0.0 1.6 %copy-start = (bf16[1,128,8192]{2,1,0:T(8,128)(2,1)S(1)}, bf16[1,128,8192]{2,1,0:T(8,128)(2,1)}, u32[]{:S(2)}) copy-start(bf16[1,128,8192]{2,1,0:T(8,128)(2,1)} %param.5) | copy-start | bytes 6291460
  1.6 1.6 %copy-start.1 = (bf16[1,128,8192]{2,1,0:T(8,128)(2,1)S(1)}, bf16[1,128,8192]{2,1,0:T(8,128)(2,1)}, u32[]{:S(2)}) copy-start(bf16[1,128,8192]{2,1,0:T(8,128)(2,1)} %param.6) | copy-start | bytes 6291460
  3.2 0.8 %copy-start.2 = (bf16[128,128]{1,0:T(8,128)(2,1)S(1)}, bf16[128,128]{1,0:T(8,128)(2,1)}, u32[]{:S(2)}) copy-start(bf16[128,128]{1,0:T(8,128)(2,1)} %w_in.1) | copy-start | bytes 98308
  3.9 0.7 copy-start.3
  4.6 0.7 copy-start.4

commit v2 on v1

--- a/solution.py
+++ b/solution.py
@@ -37,7 +37,7 @@
 def kernel(
     hidden, values, w_in, w_beta, ids, out,
     hid, wbuf, vbuf, kown, kbuf, m_hi, m_lo, acc, lacc,
-    hid_sem, y_send, y_recv, x_send, x_recv, zr_send, zr_recv, zl_send, zl_recv,
+    wb, idm, hid_sem, w_sem, wb_sem, id_sem, y_send, y_recv, x_send, x_recv, zr_send, zr_recv, zl_send, zl_recv,
     s_send, s_recv, k_send, k_recv, v_send, v_recv, r_send, r_recv, d_send, d_recv,
 ):
     s, f = lax.axis_index("seg"), lax.axis_index("fsdp")
@@ -67,20 +67,30 @@
     for peer in peers:
         pl.semaphore_signal(barrier, inc=1, device_id=peer, device_id_type=MESH)
     hid_copy = pltpu.make_async_copy(hidden, hid, hid_sem)
+    own = wbuf.at[core, z, x]
+    owner = core == yl
+    w_copy = pltpu.make_async_copy(w_in, wbuf.at[core, z, x, pl.ds(0, 128)], w_sem)
+    wb_copy = pltpu.make_async_copy(w_beta, wb, wb_sem)
+    id_copy = pltpu.make_async_copy(ids, idm, id_sem)
+
+    @pl.when(owner)
+    def _():
+        w_copy.start()
+        wb_copy.start()
+
     hid_copy.start()
+    id_copy.start()
     for r in range(SEGS - 1):
 
         @pl.when(s <= r)
         def _(r=r):
             kbuf[r] = jnp.zeros(kbuf.shape[1:], F32)
 
-    own = wbuf.at[core, z, x]
-    owner = core == yl
-
     @pl.when(owner)
     def _():
-        wbuf[core, z, x, 0:128, :] = w_in[...]
-        wbuf[core, z, x, 128:144, :] = jnp.broadcast_to(w_beta[...], (16, 128))
+        wb_copy.wait()
+        wbuf[core, z, x, 128:144, :] = jnp.broadcast_to(wb[...], (16, 128))
+        w_copy.wait()
 
     pl.semaphore_wait(barrier, len(peers))
 
@@ -108,6 +118,7 @@
     for c in x_copies:
         c.start()
     hid_copy.wait()
+    id_copy.wait()
     acc[...] = jnp.zeros_like(acc)
     lacc[...] = jnp.zeros_like(lacc)
     for c in x_copies:
@@ -225,7 +236,7 @@
             phi = phi_of(p)
             beta = kbuf[r, 64:72, :]
             div = jnp.maximum(dot_t(jnp.broadcast_to(norm, (8, 128 * NU)), phi), 1.0)
-            keep = jnp.where((ids[0, r + 1] == ids[0, r]) | (s < r + 1), 1.0, 0.0).astype(F32)
+            keep = jnp.where((idm[0, r + 1] == idm[0, r]) | (s < r + 1), 1.0, 0.0).astype(F32)
             phis.append(phi)
             betas.append(beta[0:1])
             gains.append((beta / div)[0:1])
@@ -309,13 +320,12 @@
     _, tokens, width = hidden.shape
     chunks = width // CHUNK
     dma = pltpu.SemaphoreType.DMA
-    vmem = pl.BlockSpec(memory_space=pltpu.VMEM)
-    hbm = pl.BlockSpec(memory_space=pl.ANY)
+    hbm = pl.BlockSpec(memory_space=pltpu.HBM)
     mixed = pl.pallas_call(
         kernel,
         out_shape=jax.ShapeDtypeStruct((tokens, width), BF16),
-        in_specs=[hbm, hbm, vmem, vmem, pl.BlockSpec(memory_space=pltpu.SMEM)],
-        out_specs=vmem,
+        in_specs=[hbm] * 5,
+        out_specs=pl.BlockSpec(memory_space=pltpu.VMEM),
         scratch_shapes=[
             pltpu.VMEM((tokens, width), BF16),
             pltpu.VMEM((YL, Z, X, 144, 128), BF16),
@@ -326,7 +336,8 @@
             pltpu.VMEM((tokens, 128 * (SEGS - 1)), BF16),
             pltpu.VMEM((tokens, 128), F32),
             pltpu.VMEM((tokens, 128), F32),
-            dma, dma, dma, dma((X - 1,)), dma((X - 1,)),
+            pltpu.VMEM((1, 128), BF16), pltpu.SMEM((1, SEGS), jnp.int32),
+            dma, dma, dma, dma, dma, dma, dma((X - 1,)), dma((X - 1,)),
             dma((Z // 2,)), dma((Z // 2,)), dma((Z // 2,)), dma((Z // 2,)),
             dma((Z,)), dma((Z,)), dma((3,)), dma((SEGS - 1,)),
             dma((chunks,)), dma((chunks,)), dma((chunks,)), dma((chunks,)), dma, dma,
@@ -334,7 +345,10 @@
         compiler_params=pltpu.CompilerParams(
             collective_id=0, has_side_effects=True, vmem_limit_bytes=32 << 20
         ),
-    )(hidden[0], value_states[0], w_in, w_beta.reshape(1, 128), book_ids)
+    )(*(
+        pltpu.with_memory_space_constraint(a, pltpu.HBM)
+        for a in (hidden[0], value_states[0], w_in, w_beta.reshape(1, 128), book_ids)
+    ))
     return mixed[None]
 
 

time: 66.7 us -> 61 us (0.915)
  local copies, waits for them, and re-layouts: 6.57 us -> 1.32 us
    unnamed x11 -> x1, local copies, waits for them, and re-layouts: 6.57 us -> 1.32 us
where the time goes in v2:
time: 61 us; the launch traced here: 60.5 us
  Pallas kernels  59.2 us (97%)
  local copies, waits for them, and re-layouts  1.32 us (2%)
    pallas_call x1, Pallas kernels, per_device(): pl.pallas_call(kernel, out_shape=jax.ShapeDtypeStruct((tokens, width), BF...  59.2 us
    unnamed x1, local copies, waits for them, and re-layouts  1.32 us

profile of v2, /device:TPU:17, one launch (start us, length us, event | category | flops | bytes accessed | tf_op | source)
XLA Modules:
  0.0 60.5 jit_solution(12436140015726666762)
XLA Ops:
  0.0 59.2 %shard_map.55 = bf16[128,8192]{1,0:T(8,128)(2,1)S(1)} custom-call(bf16[128,8192]{1,0:T(8,128)(2,1)} %bitcast.5, bf16[128,8192]{1,0:T(8,128)(2,1)} %bitcast.6, bf16[128,128]{1,0:T(8,128)(2,1)} %w_in.1, bf16[1,128]{1,0:T(2,128)(2,1)} %bitcast.7, s32[1,4]{1,0:T(1,128)} %ids.1), custom_call_target="tpu_custom_call" | custom-call | tf_op jit(solution)/shard_map/pallas_call | solution.py:324
  59.2 1.3 %copy.7 = bf16[1,128,8192]{2,1,0:T(8,128)(2,1)} copy(bf16[1,128,8192]{2,1,0:T(8,128)(2,1)S(1)} %bitcast.4) | data formatting | bytes 4194304

commit v3 on v2

v3 whole, which is shorter than its diff:
```python
import functools

import jax
import jax.numpy as jnp
from jax import lax
from jax.experimental import pallas as pl
from jax.experimental.pallas import tpu as pltpu
from jax.sharding import PartitionSpec as P

NU = 3
X, Z, YL, SEGS = 4, 8, 2, 4
X_ORDER = (1, 3, 2)
CHUNK = 512
EARLY = 5
HALFWAY = 8
MESH = pl.DeviceIdType.MESH
HIGHEST = lax.Precision.HIGHEST
F32, BF16 = jnp.float32, jnp.bfloat16


def dot(a, b):
    return jnp.dot(a, b, precision=HIGHEST, preferred_element_type=F32)


def dot_t(a, b):
    return lax.dot_general(
        a, b, (((1,), (1,)), ((), ())), precision=HIGHEST, preferred_element_type=F32
    )


def halves(u, turned, low):
    return jnp.where(low, jnp.maximum(u, 0.0), jnp.maximum(-turned, 0.0))


def phi_of(p):
    return jnp.concatenate([p * pltpu.roll(p, j, 1) for j in range(1, NU + 1)], axis=1)


def kernel(
    hidden, values, w_in, w_beta, ids, out,
    hid, wbuf, vbuf, kown, kbuf, m_hi, m_lo, acc, lacc,
    wb, idm, hid_sem, w_sem, wb_sem, id_sem, y_send, y_recv, x_send, x_recv, zr_send, zr_recv, zl_send, zl_recv,
    s_send, s_recv, k_send, k_recv, v_send, v_recv, r_send, r_recv, d_send, d_recv,
):
    s, f = lax.axis_index("seg"), lax.axis_index("fsdp")
    core, yl = lax.rem(s, 2), lax.rem(f, YL)
    z = lax.rem(lax.div(f, YL), Z)
    x = lax.div(f, YL * Z)
    tokens, width = hid.shape
    chunks = width // CHUNK
    first, second = core == 0, core == 1

    def at(x_, z_, yl_):
        return (x_ * Z + z_) * YL + yl_

    sib = (s + 1 - 2 * core, f)
    cross = (lax.rem(s + 2, SEGS), f)
    y_peer = (s, at(x, z, 1 - yl))
    x_peer = [(s, at(lax.rem(x + d, X), z, yl)) for d in X_ORDER]
    right = (s, at(x, lax.rem(z + 1, Z), yl))
    left = (s, at(x, lax.rem(z + Z - 1, Z), yl))

    def remote(src, dst, send, recv, to):
        return pltpu.make_async_remote_copy(
            src_ref=src, dst_ref=dst, send_sem=send, recv_sem=recv, device_id=to, device_id_type=MESH
        )

    barrier = pltpu.get_barrier_semaphore()
    near, far = [cross, sib], [y_peer, *x_peer, right, left]

    def greet(peers):
        for peer in peers:
            pl.semaphore_signal(barrier, inc=1, device_id=peer, device_id_type=MESH)

    greet(near)
    pl.when(second)(lambda: greet(far))
    hid_copy = pltpu.make_async_copy(hidden, hid, hid_sem)
    w_copy = pltpu.make_async_copy(w_in, wbuf.at[z, x, yl, pl.ds(0, 128)], w_sem)
    wb_copy = pltpu.make_async_copy(w_beta, wb, wb_sem)
    id_copy = pltpu.make_async_copy(ids, idm, id_sem)

    @pl.when(second)
    def _():
        w_copy.start()
        wb_copy.start()

    hid_copy.start()
    id_copy.start()
    for r in range(SEGS - 1):

        @pl.when(s <= r)
        def _(r=r):
            kbuf[r] = jnp.zeros(kbuf.shape[1:], F32)

    def columns(k):
        return pl.ds(pl.multiple_of(k * CHUNK, CHUNK), CHUNK)

    def v_copy(k, slot):
        c = columns(k)
        return remote(values.at[:, c], vbuf.at[slot, :, c], v_send.at[k], v_recv.at[k], cross)

    def v_start(lo, hi, slot):
        pl.loop(lo, hi)(lambda k: v_copy(k, slot).start())

    def project(zb):
        total = jnp.zeros((tokens, 128), F32)
        gate = jnp.zeros((tokens, 128), F32)
        for xb in range(X):
            lo = pl.multiple_of(at(xb, zb, 0) * 128, 128 * YL)
            h = hid[:, pl.ds(lo, 128 * YL)]
            w = jnp.concatenate([wbuf[zb, xb, p, 0:128, :] for p in range(YL)], axis=0)
            total += jnp.dot(h, w, preferred_element_type=F32)
            for p in range(YL):
                row = wbuf[zb, xb, p, 128:144, :][0:1].astype(F32)
                gate += h[:, 128 * p : 128 * (p + 1)].astype(F32) * row
        acc[...] += total
        lacc[...] += gate

    def block(d):
        return lax.rem(z + d + Z, Z)

    half = Z // 2
    order = [0] + [d for t in range(1, half) for d in (-t, t)] + [half]

    def to_sib(i):
        b = wbuf.at[block(order[i])]
        return remote(b, b, s_send.at[i], s_recv.at[i], sib)

    def clear():
        acc[...] = jnp.zeros_like(acc)
        lacc[...] = jnp.zeros_like(lacc)
        hid_copy.wait()
        id_copy.wait()

    own = wbuf.at[z, x, yl]
    y_copy = remote(own, own, y_send, y_recv, y_peer)
    pair = wbuf.at[z, x]
    x_copies = [
        remote(pair, pair, x_send.at[i], x_recv.at[i], peer) for i, peer in enumerate(x_peer)
    ]

    def ring(t, j):
        xs = lax.rem(x + X - (0, *X_ORDER)[j], X)
        copies = []
        if t < half or j < X // 2:
            b = wbuf.at[block(1 - t), xs]
            copies.append(remote(b, b, zr_send.at[t - 1, j], zr_recv.at[t - 1, j], right))
        if t < half or j >= X // 2:
            b = wbuf.at[block(t - 1), xs]
            copies.append(remote(b, b, zl_send.at[t - 1, j], zl_recv.at[t - 1, j], left))
        return copies

    rings = {(t, j): ring(t, j) for t in range(1, half + 1) for j in range(X)}

    @pl.when(first)
    def _():
        pl.semaphore_wait(barrier, len(near))
        pl.when(s == 0)(lambda: v_start(0, chunks, 0))
        clear()
        for i in range(Z):
            to_sib(i).wait_recv()
            project(block(order[i]))

    @pl.when(second)
    def _():
        wb_copy.wait()
        wbuf[z, x, yl, 128:144, :] = jnp.broadcast_to(wb[...], (16, 128))
        w_copy.wait()
        pl.semaphore_wait(barrier, len(near) + len(far))
        y_copy.start()
        pl.when(s == 1)(lambda: v_start(0, EARLY, 1))
        y_copy.wait_recv()
        for c in x_copies:
            c.start()
        for c in rings[1, 0]:
            c.start()
        clear()
        for j in range(1, X):
            x_copies[j - 1].wait_recv()
            for c in rings[1, j]:
                c.start()
        to_sib(0).start()
        project(block(0))
        for t in range(1, half + 1):
            for j in range(X):
                for c in rings[t, j]:
                    c.wait_recv()
                if t < half:
                    for c in rings[t + 1, j]:
                        c.start()
            for i in (2 * t - 1, 2 * t):
                if i < Z:
                    to_sib(i).start()
            for i in (2 * t - 1, 2 * t):
                if i < Z:
                    project(block(order[i]))

    low = lax.broadcasted_iota(jnp.int32, (tokens, 128), 1) < 64
    low_half = low[: tokens // 2]
    proj = acc[...]
    turned = pltpu.roll(proj, 64, 1)
    logit = dot_t(jnp.ones((8, 128), F32), lacc[...])
    kown[0:64, :] = jnp.where(low_half, turned[0:64], proj[64:128])
    kown[64:72, :] = 1.0 / (1.0 + jnp.exp(-logit))

    def k_copy(src, r, i, to):
        return remote(src, kbuf.at[r], k_send.at[i], k_recv.at[r], to)

    v_sib = remote(values, vbuf.at[s], d_send, d_recv, sib)

    @pl.when(first)
    def _():
        k_copy(kown, s, 0, sib).start()
        v_sib.start()

    @pl.when(s == 1)
    def _():
        k_copy(kown, 1, 0, cross).start()
        k_copy(kown, 0, 0, sib).wait_recv()
        k_copy(kbuf.at[0], 0, 1, cross).start()
        v_start(EARLY, chunks, 1)

    phi_q = phi_of(halves(proj, turned, low))

    def relay(k, slot):
        c = columns(k)
        b = vbuf.at[slot, :, c]
        return remote(b, b, r_send.at[k], r_recv.at[k], sib)

    def take(k, slot):
        v_copy(k, slot).wait_recv()
        relay(k, slot).start()

    pl.when(s == 2)(lambda: pl.loop(0, HALFWAY)(lambda k: take(k, 0)))
    pl.when(s == 3)(lambda: pl.loop(0, EARLY)(lambda k: take(k, 1)))

    @pl.when(s == 2)
    def _():
        for r in (1, 0):
            k_copy(kown, r, 0, sib).wait_recv()

    @pl.when(s == 3)
    def _():
        for i, r in enumerate((1, 0)):
            k_copy(kown, r, 0, cross).wait_recv()
            k_copy(kbuf.at[r], r, 1 + i, sib).start()
        k_copy(kown, 2, 0, sib).wait_recv()

    @pl.when(s > 0)
    def _():
        keeps, phis, betas, gains = [], [], [], []
        norm = jnp.zeros((1, 128 * NU), F32)
        for r in range(SEGS - 1):
            two = kbuf[r, 0:64, :]
            two_turned = pltpu.roll(two, 64, 1)
            p = jnp.concatenate(
                [halves(two, two_turned, low_half), halves(two_turned, two, low_half)], axis=0
            )
            phi = phi_of(p)
            beta = kbuf[r, 64:72, :]
            div = jnp.maximum(dot_t(jnp.broadcast_to(norm, (8, 128 * NU)), phi), 1.0)
            keep = jnp.where((idm[0, r + 1] == idm[0, r]) | (s < r + 1), 1.0, 0.0).astype(F32)
            phis.append(phi)
            betas.append(beta[0:1])
            gains.append((beta / div)[0:1])
            keeps.append(keep)
            norm = keep * (norm + jnp.sum(phi, axis=0, keepdims=True))
        scale = 1.0 / jnp.maximum(jnp.sum(phi_q * norm, axis=1, keepdims=True), 1.0)
        q = phi_q
        for r in reversed(range(SEGS - 1)):
            q = keeps[r] * q
            t = dot_t(q, phis[r])
            m = t * betas[r] * scale
            hi = m.astype(BF16)
            m_hi[:, 128 * r : 128 * (r + 1)] = hi
            m_lo[:, 128 * r : 128 * (r + 1)] = (m - hi.astype(F32)).astype(BF16)
            if r:
                q = q - dot(t * gains[r], phis[r])

    def mix(k, n):
        c = columns(k)
        v = vbuf[0:n, :, c].reshape(128 * n, CHUNK)
        mixed = jnp.dot(m_hi[:, : 128 * n], v, preferred_element_type=F32)
        mixed += jnp.dot(m_lo[:, : 128 * n], v, preferred_element_type=F32)
        out[:, c] = mixed.astype(BF16)

    @pl.when(s == 0)
    def _():
        out[...] = jnp.zeros_like(out)

    @pl.when(s == 1)
    def _():
        remote(values, vbuf.at[0], d_send, d_recv, sib).wait_recv()
        pl.loop(0, chunks)(lambda k: mix(k, 1))

    @pl.when(s == 2)
    def _():
        pl.loop(HALFWAY, chunks)(lambda k: take(k, 0))

        @pl.loop(0, chunks)
        def _(k):
            relay(k, 1).wait_recv()
            mix(k, 2)

        pl.loop(0, chunks)(lambda k: relay(k, 0).wait_send())

    @pl.when(s == 3)
    def _():
        remote(values, vbuf.at[2], d_send, d_recv, sib).wait_recv()

        @pl.loop(0, EARLY)
        def _(k):
            relay(k, 0).wait_recv()
            mix(k, 3)

        @pl.loop(EARLY, chunks)
        def _(k):
            take(k, 1)
            relay(k, 0).wait_recv()
            mix(k, 3)

        pl.loop(0, chunks)(lambda k: relay(k, 1).wait_send())

    @pl.when(first)
    def _():
        k_copy(kown, s, 0, sib).wait_send()
        v_sib.wait_send()

    @pl.when(second)
    def _():
        y_copy.wait_send()
        for c in (*x_copies, *sum(rings.values(), []), *(to_sib(i) for i in range(Z))):
            c.wait_send()

    @pl.when(s < 2)
    def _():
        pl.loop(0, chunks)(lambda k: v_copy(k, s).wait_send())

    @pl.when(s == 1)
    def _():
        k_copy(kown, 1, 0, cross).wait_send()
        k_copy(kbuf.at[0], 0, 1, cross).wait_send()

    @pl.when(s == 3)
    def _():
        for i, r in enumerate((1, 0)):
            k_copy(kbuf.at[r], r, 1 + i, sib).wait_send()


def per_device(hidden, value_states, w_in, w_beta, book_ids):
    _, tokens, width = hidden.shape
    chunks = width // CHUNK
    dma = pltpu.SemaphoreType.DMA
    hbm = pl.BlockSpec(memory_space=pltpu.HBM)
    mixed = pl.pallas_call(
        kernel,
        out_shape=jax.ShapeDtypeStruct((tokens, width), BF16),
        in_specs=[hbm] * 5,
        out_specs=pl.BlockSpec(memory_space=pltpu.VMEM),
        scratch_shapes=[
            pltpu.VMEM((tokens, width), BF16),
            pltpu.VMEM((Z, X, YL, 144, 128), BF16),
            pltpu.VMEM((SEGS - 1, tokens, width), BF16),
            pltpu.VMEM((72, 128), F32),
            pltpu.VMEM((SEGS - 1, 72, 128), F32),
            pltpu.VMEM((tokens, 128 * (SEGS - 1)), BF16),
            pltpu.VMEM((tokens, 128 * (SEGS - 1)), BF16),
            pltpu.VMEM((tokens, 128), F32),
            pltpu.VMEM((tokens, 128), F32),
            pltpu.VMEM((1, 128), BF16), pltpu.SMEM((1, SEGS), jnp.int32),
            dma, dma, dma, dma, dma, dma, dma((X - 1,)), dma((X - 1,)),
            dma((Z // 2, X)), dma((Z // 2, X)), dma((Z // 2, X)), dma((Z // 2, X)),
            dma((Z,)), dma((Z,)), dma((3,)), dma((SEGS - 1,)),
            dma((chunks,)), dma((chunks,)), dma((chunks,)), dma((chunks,)), dma, dma,
        ],
        compiler_params=pltpu.CompilerParams(
            collective_id=0, has_side_effects=True, vmem_limit_bytes=32 << 20
        ),
    )(*(
        pltpu.with_memory_space_constraint(a, pltpu.HBM)
        for a in (hidden[0], value_states[0], w_in, w_beta.reshape(1, 128), book_ids)
    ))
    return mixed[None]


def solution(mesh):
    return jax.shard_map(
        per_device,
        mesh=mesh,
        in_specs=(
            P("fsdp", "seg", None),
            P("fsdp", "seg", None),
            P("fsdp", None),
            P("fsdp"),
            P("fsdp", None),
        ),
        out_specs=P("fsdp", "seg", None),
        check_vma=False,
    )
```

time: 61 us -> 55.4 us (0.908)
  Pallas kernels: 59.2 us -> 53.9 us
    pallas_call x1, Pallas kernels: 59.2 us -> 53.9 us  [per_device(): pl.pallas_call(kernel, out_shape=jax.ShapeDtypeStruct((tokens, width), BF...]
where the time goes in v3:
time: 55.4 us; the launch traced here: 55.2 us
  Pallas kernels  53.9 us (97%)
  local copies, waits for them, and re-layouts  1.32 us (2%)
    pallas_call x1, Pallas kernels, per_device(): pl.pallas_call(kernel, out_shape=jax.ShapeDtypeStruct((tokens, width), BF...  53.9 us
    unnamed x1, local copies, waits for them, and re-layouts  1.32 us

profile of v3, /device:TPU:17, one launch (start us, length us, event | category | flops | bytes accessed | tf_op | source)
XLA Modules:
  0.0 55.2 jit_solution(2603460779529140021)
XLA Ops:
  0.0 53.9 %shard_map.55 = bf16[128,8192]{1,0:T(8,128)(2,1)S(1)} custom-call(bf16[128,8192]{1,0:T(8,128)(2,1)} %bitcast.5, bf16[128,8192]{1,0:T(8,128)(2,1)} %bitcast.6, bf16[128,128]{1,0:T(8,128)(2,1)} %w_in.1, bf16[1,128]{1,0:T(2,128)(2,1)} %bitcast.7, s32[1,4]{1,0:T(1,128)} %ids.1), custom_call_target="tpu_custom_call" | custom-call | tf_op jit(solution)/shard_map/pallas_call | solution.py:355
  53.9 1.3 %copy.7 = bf16[1,128,8192]{2,1,0:T(8,128)(2,1)} copy(bf16[1,128,8192]{2,1,0:T(8,128)(2,1)S(1)} %bitcast.4) | data formatting | bytes 4194304

commit v4 on v3

v4 whole, which is shorter than its diff:
```python
import functools

import jax
import jax.numpy as jnp
from jax import lax
from jax.experimental import pallas as pl
from jax.experimental.pallas import tpu as pltpu
from jax.sharding import PartitionSpec as P

NU = 3
X, Z, YL, SEGS = 4, 8, 2, 4
X_ORDER = (1, 3, 2)
GROUPS = ((0, 16, 512),)
CHUNKS = 16
EARLY = 8
HALFWAY = 8
MESH = pl.DeviceIdType.MESH
HIGHEST = lax.Precision.HIGHEST
F32, BF16 = jnp.float32, jnp.bfloat16


def dot(a, b):
    return jnp.dot(a, b, precision=HIGHEST, preferred_element_type=F32)


def dot_t(a, b):
    return lax.dot_general(
        a, b, (((1,), (1,)), ((), ())), precision=HIGHEST, preferred_element_type=F32
    )


def halves(u, turned, low):
    return jnp.where(low, jnp.maximum(u, 0.0), jnp.maximum(-turned, 0.0))


def phi_of(p):
    return jnp.concatenate([p * pltpu.roll(p, j, 1) for j in range(1, NU + 1)], axis=1)


def kernel(
    hidden, values, w_in, w_beta, ids, out,
    hid, wbuf, vbuf, kown, kbuf, m_hi, m_lo, acc, lacc,
    wb, idm, hid_sem, w_sem, wb_sem, id_sem, y_send, y_recv, x_send, x_recv, ring_send, zr_recv, zl_recv,
    s_send, s_recv, k_send, k_recv, v_send, v_recv, r_send, r_recv, d_send, d_recv,
):
    s, f = lax.axis_index("seg"), lax.axis_index("fsdp")
    core, yl = lax.rem(s, 2), lax.rem(f, YL)
    z = lax.rem(lax.div(f, YL), Z)
    x = lax.div(f, YL * Z)
    tokens = hid.shape[0]
    first, second = core == 0, core == 1

    def at(x_, z_, yl_):
        return (x_ * Z + z_) * YL + yl_

    sib = (s + 1 - 2 * core, f)
    cross = (lax.rem(s + 2, SEGS), f)
    y_peer = (s, at(x, z, 1 - yl))
    y_cross = (lax.rem(s + 2, SEGS), at(x, z, 1 - yl))
    x_peer = [(s, at(lax.rem(x + d, X), z, yl)) for d in X_ORDER]
    right = (s, at(x, lax.rem(z + 1, Z), yl))
    left = (s, at(x, lax.rem(z + Z - 1, Z), yl))

    def remote(src, dst, send, recv, to):
        return pltpu.make_async_remote_copy(
            src_ref=src, dst_ref=dst, send_sem=send, recv_sem=recv, device_id=to, device_id_type=MESH
        )

    barrier = pltpu.get_barrier_semaphore()
    near, far = [cross, sib], [y_cross, *x_peer, right, left]

    def greet(peers):
        for peer in peers:
            pl.semaphore_signal(barrier, inc=1, device_id=peer, device_id_type=MESH)

    greet(near)
    pl.when(second)(lambda: greet(far))
    pl.when(s == 3)(lambda: greet([y_peer]))
    hid_copy = pltpu.make_async_copy(hidden, hid, hid_sem)
    w_copy = pltpu.make_async_copy(w_in, wbuf.at[z, x, yl, pl.ds(0, 128)], w_sem)
    wb_copy = pltpu.make_async_copy(w_beta, wb, wb_sem)
    id_copy = pltpu.make_async_copy(ids, idm, id_sem)

    @pl.when(second)
    def _():
        w_copy.start()
        wb_copy.start()

    hid_copy.start()
    id_copy.start()
    for r in range(SEGS - 1):

        @pl.when(s <= r)
        def _(r=r):
            kbuf[r] = jnp.zeros(kbuf.shape[1:], BF16)

    def each(lo, hi, body):
        for start, count, wide in GROUPS:
            col0 = sum(min(max(start - a, 0), n) * w for a, n, w in GROUPS)
            a, b = max(lo, start), min(hi, start + count)
            if a < b:

                @pl.loop(a, b)
                def _(k):
                    body(k, pl.ds(pl.multiple_of(col0 + (k - start) * wide, 256), wide), wide)

    def v_copy(k, c, slot):
        return remote(values.at[:, c], vbuf.at[slot, :, c], v_send, v_recv.at[k], cross)

    def v_start(lo, hi, slot):
        each(lo, hi, lambda k, c, _: v_copy(k, c, slot).start())

    def project(zb):
        total = jnp.zeros((tokens, 128), F32)
        gate = jnp.zeros((tokens, 128), F32)
        for xb in range(X):
            lo = pl.multiple_of(at(xb, zb, 0) * 128, 128 * YL)
            h = hid[:, pl.ds(lo, 128 * YL)]
            w = jnp.concatenate([wbuf[zb, xb, p, 0:128, :] for p in range(YL)], axis=0)
            total += jnp.dot(h, w, preferred_element_type=F32)
            for p in range(YL):
                row = wbuf[zb, xb, p, 128:144, :][0:1].astype(F32)
                gate += h[:, 128 * p : 128 * (p + 1)].astype(F32) * row
        acc[...] += total
        lacc[...] += gate

    def block(d):
        return lax.rem(z + d + Z, Z)

    half = Z // 2
    order = [0] + [d for t in range(1, half) for d in (-t, t)] + [half]

    def to_sib(i):
        b = wbuf.at[block(order[i])]
        return remote(b, b, s_send, s_recv.at[(i + 1) // 2], sib)

    def took(n, sem):
        b = wbuf.at[pl.ds(0, n)]
        remote(b, b, s_send, s_recv.at[sem], sib).wait_recv()

    def clear():
        acc[...] = jnp.zeros_like(acc)
        lacc[...] = jnp.zeros_like(lacc)
        hid_copy.wait()
        id_copy.wait()

    own, pair = wbuf.at[z, x, yl], wbuf.at[z, x]
    y_copies = [remote(own, own, y_send, y_recv, to) for to in (y_peer, y_cross)]
    x_copies = [remote(pair, pair, x_send, x_recv, peer) for peer in x_peer]

    def ring(t, j):
        xs, g = lax.rem(x + X - (0, *X_ORDER)[j], X), min(j, 1)
        if t < half or j < X // 2:
            b = wbuf.at[block(1 - t), xs]
            remote(b, b, ring_send, zr_recv.at[t - 1, g], right).start()
        if t < half or j >= X // 2:
            b = wbuf.at[block(t - 1), xs]
            remote(b, b, ring_send, zl_recv.at[t - 1, g], left).start()

    def came(t, g):
        for sem, n in (
            (zr_recv, (1, 3)[g] if t < half else 1),
            (zl_recv, (1, 3)[g] if t < half else 2 * g),
        ):
            if n:
                b = wbuf.at[0, pl.ds(0, n)]
                remote(b, b, ring_send, sem.at[t - 1, g], left).wait_recv()

    @pl.when(first)
    def _():
        pl.semaphore_wait(barrier, len(near))
        pl.when(s == 0)(lambda: v_start(0, CHUNKS, 0))
        clear()
        for sem in range(half + 1):
            blocks = [i for i in range(Z) if (i + 1) // 2 == sem]
            took(len(blocks), sem)
            for i in blocks:
                project(block(order[i]))

    @pl.when(second)
    def _():
        wb_copy.wait()
        wbuf[z, x, yl, 128:144, :] = jnp.broadcast_to(wb[...], (16, 128))
        w_copy.wait()

        @pl.when(s == 1)
        def _():
            pl.semaphore_wait(barrier, len(near) + len(far))
            v_start(0, EARLY, 1)

        @pl.when(s == 3)
        def _():
            pl.semaphore_wait(barrier, len(near) + len(far) + 1)
            for c in y_copies:
                c.start()

        y_copies[0].wait_recv()
        for c in x_copies:
            c.start()
        ring(1, 0)
        clear()
        b = wbuf.at[0, pl.ds(0, X - 1)]
        remote(b, b, x_send, x_recv, sib).wait_recv()
        for j in range(1, X):
            ring(1, j)
        to_sib(0).start()
        project(block(0))
        for t in range(1, half + 1):
            for g in range(2):
                came(t, g)
                if t < half:
                    for j in ((0,), (1, 2, 3))[g]:
                        ring(t + 1, j)
            fresh = [i for i in (2 * t - 1, 2 * t) if i < Z]
            for i in fresh:
                to_sib(i).start()
            for i in fresh:
                project(block(order[i]))

    low = lax.broadcasted_iota(jnp.int32, (tokens, 128), 1) < 64
    low_half = low[: tokens // 2]
    proj = acc[...]
    turned = pltpu.roll(proj, 64, 1)
    logit = dot_t(jnp.ones((8, 128), F32), lacc[...])
    gate = 1.0 / (1.0 + jnp.exp(-logit))
    gate_hi = gate.astype(BF16)
    gate_lo = (gate - gate_hi.astype(F32)).astype(BF16)
    kown[0:64, :] = jnp.where(low_half, turned[0:64], proj[64:128]).astype(BF16)
    kown[64:80, :] = jnp.concatenate([gate_hi, gate_lo], axis=0)

    def k_copy(src, r, to):
        return remote(src, kbuf.at[r], k_send, k_recv.at[r], to)

    v_sib = remote(values, vbuf.at[s], d_send, d_recv, sib)

    @pl.when(first)
    def _():
        k_copy(kown, s, sib).start()
        v_sib.start()

    @pl.when(s == 1)
    def _():
        k_copy(kown, 1, cross).start()
        k_copy(kown, 0, sib).wait_recv()
        k_copy(kbuf.at[0], 0, cross).start()
        v_start(EARLY, CHUNKS, 1)

    phi_q = phi_of(halves(proj, turned, low))

    def relay(k, c, slot):
        b = vbuf.at[slot, :, c]
        return remote(b, b, r_send, r_recv.at[k], sib)

    def take(k, c, slot):
        v_copy(k, c, slot).wait_recv()
        relay(k, c, slot).start()

    pl.when(s == 2)(lambda: each(0, HALFWAY, lambda k, c, _: take(k, c, 0)))
    pl.when(s == 3)(lambda: each(0, EARLY, lambda k, c, _: take(k, c, 1)))

    @pl.when(s == 2)
    def _():
        for r in (1, 0):
            k_copy(kown, r, sib).wait_recv()

    @pl.when(s == 3)
    def _():
        for r in (1, 0):
            k_copy(kown, r, cross).wait_recv()
            k_copy(kbuf.at[r], r, sib).start()
        k_copy(kown, 2, sib).wait_recv()

    @pl.when(s > 0)
    def _():
        keeps, phis, betas, gains = [], [], [], []
        norm = jnp.zeros((1, 128 * NU), F32)
        for r in range(SEGS - 1):
            two = kbuf[r, 0:64, :].astype(F32)
            two_turned = pltpu.roll(two, 64, 1)
            p = jnp.concatenate(
                [halves(two, two_turned, low_half), halves(two_turned, two, low_half)], axis=0
            )
            phi = phi_of(p)
            gates = kbuf[r, 64:80, :].astype(F32)
            beta = gates[0:8] + gates[8:16]
            div = jnp.maximum(dot_t(jnp.broadcast_to(norm, (8, 128 * NU)), phi), 1.0)
            keep = jnp.where((idm[0, r + 1] == idm[0, r]) | (s < r + 1), 1.0, 0.0).astype(F32)
            phis.append(phi)
            betas.append(beta[0:1])
            gains.append((beta / div)[0:1])
            keeps.append(keep)
            norm = keep * (norm + jnp.sum(phi, axis=0, keepdims=True))
        scale = 1.0 / jnp.maximum(jnp.sum(phi_q * norm, axis=1, keepdims=True), 1.0)
        q = phi_q
        for r in reversed(range(SEGS - 1)):
            q = keeps[r] * q
            t = dot_t(q, phis[r])
            m = t * betas[r] * scale
            hi = m.astype(BF16)
            m_hi[:, 128 * r : 128 * (r + 1)] = hi
            m_lo[:, 128 * r : 128 * (r + 1)] = (m - hi.astype(F32)).astype(BF16)
            if r:
                q = q - dot(t * gains[r], phis[r])

    def mix(c, wide, n):
        v = vbuf[0:n, :, c].reshape(128 * n, wide)
        mixed = jnp.dot(m_hi[:, : 128 * n], v, preferred_element_type=F32)
        mixed += jnp.dot(m_lo[:, : 128 * n], v, preferred_element_type=F32)
        out[:, c] = mixed.astype(BF16)

    @pl.when(s == 0)
    def _():
        out[...] = jnp.zeros_like(out)

    @pl.when(s == 1)
    def _():
        remote(values, vbuf.at[0], d_send, d_recv, sib).wait_recv()
        each(0, CHUNKS, lambda k, c, wide: mix(c, wide, 1))

    def last(slot, n, taken):
        def use(k, c, wide):
            relay(k, c, 1 - slot).wait_recv()
            mix(c, wide, n)

        def take_use(k, c, wide):
            take(k, c, slot)
            use(k, c, wide)

        each(0, taken, use)
        each(taken, CHUNKS, take_use)
        relay(0, slice(None), slot).wait_send()

    @pl.when(s == 2)
    def _():
        last(0, 2, HALFWAY)

    @pl.when(s == 3)
    def _():
        remote(values, vbuf.at[2], d_send, d_recv, sib).wait_recv()
        last(1, 3, EARLY)

    @pl.when(first)
    def _():
        k_copy(kown, s, sib).wait_send()
        v_sib.wait_send()

    @pl.when(second)
    def _():
        for n, sem in ((Z - 1, ring_send), (Z, s_send)):
            b = wbuf.at[pl.ds(0, n)]
            remote(b, b, sem, s_recv.at[0], sib).wait_send()
        b = wbuf.at[0, pl.ds(0, X - 1)]
        remote(b, b, x_send, x_recv, sib).wait_send()
        b = kbuf.at[pl.ds(0, 2)]
        remote(b, b, k_send, k_recv.at[0], sib).wait_send()

    @pl.when(s == 3)
    def _():
        remote(pair, pair, y_send, y_recv, sib).wait_send()

    @pl.when(s < 2)
    def _():
        remote(values, vbuf.at[0], v_send, v_recv.at[0], cross).wait_send()


def per_device(hidden, value_states, w_in, w_beta, book_ids):
    _, tokens, width = hidden.shape
    dma = pltpu.SemaphoreType.DMA
    hbm = pl.BlockSpec(memory_space=pltpu.HBM)
    mixed = pl.pallas_call(
        kernel,
        out_shape=jax.ShapeDtypeStruct((tokens, width), BF16),
        in_specs=[hbm] * 5,
        out_specs=pl.BlockSpec(memory_space=pltpu.VMEM),
        scratch_shapes=[
            pltpu.VMEM((tokens, width), BF16),
            pltpu.VMEM((Z, X, YL, 144, 128), BF16),
            pltpu.VMEM((SEGS - 1, tokens, width), BF16),
            pltpu.VMEM((80, 128), BF16),
            pltpu.VMEM((SEGS - 1, 80, 128), BF16),
            pltpu.VMEM((tokens, 128 * (SEGS - 1)), BF16),
            pltpu.VMEM((tokens, 128 * (SEGS - 1)), BF16),
            pltpu.VMEM((tokens, 128), F32),
            pltpu.VMEM((tokens, 128), F32),
            pltpu.VMEM((1, 128), BF16), pltpu.SMEM((1, SEGS), jnp.int32),
            dma, dma, dma, dma, dma, dma, dma, dma, dma, dma((Z // 2, 2)), dma((Z // 2, 2)),
            dma, dma((Z // 2 + 1,)), dma, dma((SEGS - 1,)),
            dma, dma((CHUNKS,)), dma, dma((CHUNKS,)), dma, dma,
        ],
        compiler_params=pltpu.CompilerParams(
            collective_id=0, has_side_effects=True, vmem_limit_bytes=32 << 20
        ),
    )(*(
        pltpu.with_memory_space_constraint(a, pltpu.HBM)
        for a in (hidden[0], value_states[0], w_in, w_beta.reshape(1, 128), book_ids)
    ))
    return mixed[None]


def solution(mesh):
    return jax.shard_map(
        per_device,
        mesh=mesh,
        in_specs=(
            P("fsdp", "seg", None),
            P("fsdp", "seg", None),
            P("fsdp", None),
            P("fsdp"),
            P("fsdp", None),
        ),
        out_specs=P("fsdp", "seg", None),
        check_vma=False,
    )
```

time: 55.4 us -> 54.4 us (0.982)
  Pallas kernels: 53.9 us -> 52.9 us
    pallas_call x1, Pallas kernels: 53.9 us -> 52.9 us  [per_device(): pl.pallas_call(kernel, out_shape=jax.ShapeDtypeStruct((tokens, width), BF...]
where the time goes in v4:
time: 54.4 us; the launch traced here: 54.3 us
  Pallas kernels  52.9 us (97%)
  local copies, waits for them, and re-layouts  1.32 us (2%)
    pallas_call x1, Pallas kernels, per_device(): pl.pallas_call(kernel, out_shape=jax.ShapeDtypeStruct((tokens, width), BF...  52.9 us
    unnamed x1, local copies, waits for them, and re-layouts  1.32 us

profile of v4, /device:TPU:17, one launch (start us, length us, event | category | flops | bytes accessed | tf_op | source)
XLA Modules:
  0.0 54.3 jit_solution(13398484341755890541)
XLA Ops:
  0.0 52.9 %shard_map.55 = bf16[128,8192]{1,0:T(8,128)(2,1)S(1)} custom-call(bf16[128,8192]{1,0:T(8,128)(2,1)} %bitcast.5, bf16[128,8192]{1,0:T(8,128)(2,1)} %bitcast.6, bf16[128,128]{1,0:T(8,128)(2,1)} %w_in.1, bf16[1,128]{1,0:T(2,128)(2,1)} %bitcast.7, s32[1,4]{1,0:T(1,128)} %ids.1), custom_call_target="tpu_custom_call" | custom-call | tf_op jit(solution)/shard_map/pallas_call | solution.py:370
  52.9 1.3 %copy.7 = bf16[1,128,8192]{2,1,0:T(8,128)(2,1)} copy(bf16[1,128,8192]{2,1,0:T(8,128)(2,1)S(1)} %bitcast.4) | data formatting | bytes 4194304

commit v5 on v4

--- a/solution.py
+++ b/solution.py
@@ -12,7 +12,7 @@
 X_ORDER = (1, 3, 2)
 GROUPS = ((0, 16, 512),)
 CHUNKS = 16
-EARLY = 8
+EARLY = 10
 HALFWAY = 8
 MESH = pl.DeviceIdType.MESH
 HIGHEST = lax.Precision.HIGHEST
@@ -39,8 +39,8 @@
 
 def kernel(
     hidden, values, w_in, w_beta, ids, out,
-    hid, wbuf, vbuf, kown, kbuf, m_hi, m_lo, acc, lacc,
-    wb, idm, hid_sem, w_sem, wb_sem, id_sem, y_send, y_recv, x_send, x_recv, ring_send, zr_recv, zl_recv,
+    hid, wbuf, vbuf, kown, kbuf, mats, acc, lacc,
+    wb, idm, ready, go, hid_sem, w_sem, wb_sem, id_sem, y_send, y_recv, x_send, x_recv, ring_send, zr_recv, zl_recv,
     s_send, s_recv, k_send, k_recv, v_send, v_recv, r_send, r_recv, d_send, d_recv,
 ):
     s, f = lax.axis_index("seg"), lax.axis_index("fsdp")
@@ -67,15 +67,14 @@
         )
 
     barrier = pltpu.get_barrier_semaphore()
-    near, far = [cross, sib], [y_cross, *x_peer, right, left]
+    near, far = [cross, sib], [y_peer, *x_peer, right, left]
 
     def greet(peers):
         for peer in peers:
             pl.semaphore_signal(barrier, inc=1, device_id=peer, device_id_type=MESH)
 
     greet(near)
-    pl.when(second)(lambda: greet(far))
-    pl.when(s == 3)(lambda: greet([y_peer]))
+    pl.when(s == 3)(lambda: greet(far))
     hid_copy = pltpu.make_async_copy(hidden, hid, hid_sem)
     w_copy = pltpu.make_async_copy(w_in, wbuf.at[z, x, yl, pl.ds(0, 128)], w_sem)
     wb_copy = pltpu.make_async_copy(w_beta, wb, wb_sem)
@@ -185,14 +184,19 @@
 
         @pl.when(s == 1)
         def _():
-            pl.semaphore_wait(barrier, len(near) + len(far))
+            pl.semaphore_wait(barrier, len(near))
             v_start(0, EARLY, 1)
+            pl.semaphore_wait(go, 1)
 
         @pl.when(s == 3)
         def _():
-            pl.semaphore_wait(barrier, len(near) + len(far) + 1)
-            for c in y_copies:
-                c.start()
+            pl.semaphore_wait(barrier, len(near) + len(far))
+            y_copies[0].start()
+            for peer in far:
+                pl.semaphore_signal(ready, inc=1, device_id=peer, device_id_type=MESH)
+            pl.semaphore_wait(ready, len(far))
+            pl.semaphore_signal(go, inc=1, device_id=cross, device_id_type=MESH)
+            y_copies[1].start()
 
         y_copies[0].wait_recv()
         for c in x_copies:
@@ -296,16 +300,13 @@
             q = keeps[r] * q
             t = dot_t(q, phis[r])
             m = t * betas[r] * scale
-            hi = m.astype(BF16)
-            m_hi[:, 128 * r : 128 * (r + 1)] = hi
-            m_lo[:, 128 * r : 128 * (r + 1)] = (m - hi.astype(F32)).astype(BF16)
+            mats[:, 128 * r : 128 * (r + 1)] = m.astype(BF16)
             if r:
                 q = q - dot(t * gains[r], phis[r])
 
     def mix(c, wide, n):
         v = vbuf[0:n, :, c].reshape(128 * n, wide)
-        mixed = jnp.dot(m_hi[:, : 128 * n], v, preferred_element_type=F32)
-        mixed += jnp.dot(m_lo[:, : 128 * n], v, preferred_element_type=F32)
+        mixed = jnp.dot(mats[:, : 128 * n], v, preferred_element_type=F32)
         out[:, c] = mixed.astype(BF16)
 
     @pl.when(s == 0)
@@ -379,10 +380,10 @@
             pltpu.VMEM((80, 128), BF16),
             pltpu.VMEM((SEGS - 1, 80, 128), BF16),
             pltpu.VMEM((tokens, 128 * (SEGS - 1)), BF16),
-            pltpu.VMEM((tokens, 128 * (SEGS - 1)), BF16),
             pltpu.VMEM((tokens, 128), F32),
             pltpu.VMEM((tokens, 128), F32),
             pltpu.VMEM((1, 128), BF16), pltpu.SMEM((1, SEGS), jnp.int32),
+            pltpu.SemaphoreType.REGULAR, pltpu.SemaphoreType.REGULAR,
             dma, dma, dma, dma, dma, dma, dma, dma, dma, dma((Z // 2, 2)), dma((Z // 2, 2)),
             dma, dma((Z // 2 + 1,)), dma, dma((SEGS - 1,)),
             dma, dma((CHUNKS,)), dma, dma((CHUNKS,)), dma, dma,

time: 54.4 us -> 53.9 us (level)
  no operation moved by 1% of the time
where the time goes in v5:
time: 53.9 us; the launch traced here: 53.8 us
  Pallas kernels  52.4 us (97%)
  local copies, waits for them, and re-layouts  1.32 us (2%)
    pallas_call x1, Pallas kernels, per_device(): pl.pallas_call(kernel, out_shape=jax.ShapeDtypeStruct((tokens, width), BF...  52.4 us
    unnamed x1, local copies, waits for them, and re-layouts  1.32 us

profile of v5, /device:TPU:17, one launch (start us, length us, event | category | flops | bytes accessed | tf_op | source)
XLA Modules:
  0.0 53.8 jit_solution(10679370731035181711)
XLA Ops:
  0.0 52.4 %shard_map.55 = bf16[128,8192]{1,0:T(8,128)(2,1)S(1)} custom-call(bf16[128,8192]{1,0:T(8,128)(2,1)} %bitcast.5, bf16[128,8192]{1,0:T(8,128)(2,1)} %bitcast.6, bf16[128,128]{1,0:T(8,128)(2,1)} %w_in.1, bf16[1,128]{1,0:T(2,128)(2,1)} %bitcast.7, s32[1,4]{1,0:T(1,128)} %ids.1), custom_call_target="tpu_custom_call" | custom-call | tf_op jit(solution)/shard_map/pallas_call | solution.py:371
  52.4 1.3 %copy.7 = bf16[1,128,8192]{2,1,0:T(8,128)(2,1)} copy(bf16[1,128,8192]{2,1,0:T(8,128)(2,1)S(1)} %bitcast.4) | data formatting | bytes 4194304

commit v6 on v5

--- a/solution.py
+++ b/solution.py
@@ -10,23 +10,31 @@
 NU = 3
 X, Z, YL, SEGS = 4, 8, 2, 4
 X_ORDER = (1, 3, 2)
-GROUPS = ((0, 16, 512),)
-CHUNKS = 16
-EARLY = 10
-HALFWAY = 8
+GROUPS = ((0, 1, 4096), (1, 8, 512))
+CHUNKS = 9
+EARLY = 2
+HALFWAY = 2
+STEP = 512
 MESH = pl.DeviceIdType.MESH
-HIGHEST = lax.Precision.HIGHEST
 F32, BF16 = jnp.float32, jnp.bfloat16
 
 
-def dot(a, b):
-    return jnp.dot(a, b, precision=HIGHEST, preferred_element_type=F32)
+def parts(a):
+    high = a.astype(BF16)
+    return high, (a - high.astype(F32)).astype(BF16)
+
+
+def dot(a, b, dims=(((1,), (0,)), ((), ()))):
+    (a_hi, a_lo), (b_hi, b_lo) = parts(a), parts(b)
+
+    def one(x, y):
+        return lax.dot_general(x, y, dims, preferred_element_type=F32)
+
+    return one(a_hi, b_hi) + (one(a_hi, b_lo) + one(a_lo, b_hi))
 
 
 def dot_t(a, b):
-    return lax.dot_general(
-        a, b, (((1,), (1,)), ((), ())), precision=HIGHEST, preferred_element_type=F32
-    )
+    return dot(a, b, (((1,), (1,)), ((), ())))
 
 
 def halves(u, turned, low):
@@ -227,10 +235,8 @@
     turned = pltpu.roll(proj, 64, 1)
     logit = dot_t(jnp.ones((8, 128), F32), lacc[...])
     gate = 1.0 / (1.0 + jnp.exp(-logit))
-    gate_hi = gate.astype(BF16)
-    gate_lo = (gate - gate_hi.astype(F32)).astype(BF16)
     kown[0:64, :] = jnp.where(low_half, turned[0:64], proj[64:128]).astype(BF16)
-    kown[64:80, :] = jnp.concatenate([gate_hi, gate_lo], axis=0)
+    kown[64:80, :] = jnp.concatenate(parts(gate), axis=0)
 
     def k_copy(src, r, to):
         return remote(src, kbuf.at[r], k_send, k_recv.at[r], to)
@@ -287,11 +293,12 @@
             phi = phi_of(p)
             gates = kbuf[r, 64:80, :].astype(F32)
             beta = gates[0:8] + gates[8:16]
-            div = jnp.maximum(dot_t(jnp.broadcast_to(norm, (8, 128 * NU)), phi), 1.0)
+            if r:
+                div = jnp.maximum(dot_t(jnp.broadcast_to(norm, (8, 128 * NU)), phi), 1.0)
             keep = jnp.where((idm[0, r + 1] == idm[0, r]) | (s < r + 1), 1.0, 0.0).astype(F32)
             phis.append(phi)
             betas.append(beta[0:1])
-            gains.append((beta / div)[0:1])
+            gains.append((beta / div)[0:1] if r else None)
             keeps.append(keep)
             norm = keep * (norm + jnp.sum(phi, axis=0, keepdims=True))
         scale = 1.0 / jnp.maximum(jnp.sum(phi_q * norm, axis=1, keepdims=True), 1.0)
@@ -304,10 +311,18 @@
             if r:
                 q = q - dot(t * gains[r], phis[r])
 
+    def mix_step(c, wide, n):
+        v = vbuf[0:n, :, c].reshape(128 * n, wide)
+        out[:, c] = jnp.dot(mats[:, : 128 * n], v, preferred_element_type=F32).astype(BF16)
+
     def mix(c, wide, n):
-        v = vbuf[0:n, :, c].reshape(128 * n, wide)
-        mixed = jnp.dot(mats[:, : 128 * n], v, preferred_element_type=F32)
-        out[:, c] = mixed.astype(BF16)
+        if wide <= STEP:
+            mix_step(c, wide, n)
+        else:
+
+            @pl.loop(0, wide // STEP)
+            def _(i):
+                mix_step(pl.ds(pl.multiple_of(c.start + i * STEP, 256), STEP), STEP, n)
 
     @pl.when(s == 0)
     def _():
@@ -318,27 +333,33 @@
         remote(values, vbuf.at[0], d_send, d_recv, sib).wait_recv()
         each(0, CHUNKS, lambda k, c, wide: mix(c, wide, 1))
 
-    def last(slot, n, taken):
-        def use(k, c, wide):
-            relay(k, c, 1 - slot).wait_recv()
-            mix(c, wide, n)
-
-        def take_use(k, c, wide):
-            take(k, c, slot)
-            use(k, c, wide)
-
-        each(0, taken, use)
-        each(taken, CHUNKS, take_use)
-        relay(0, slice(None), slot).wait_send()
+    def use(k, c, wide, slot, n):
+        relay(k, c, 1 - slot).wait_recv()
+        mix(c, wide, n)
 
     @pl.when(s == 2)
     def _():
-        last(0, 2, HALFWAY)
+        each(0, HALFWAY - 1, lambda k, c, wide: use(k, c, wide, 0, 2))
+
+        def body(k, c, wide):
+            take(k, c, 0)
+            use(k - 1, pl.ds(pl.multiple_of(c.start - wide, 256), wide), wide, 0, 2)
+
+        each(HALFWAY, CHUNKS, body)
+        each(CHUNKS - 1, CHUNKS, lambda k, c, wide: use(k, c, wide, 0, 2))
+        relay(0, slice(None), 0).wait_send()
 
     @pl.when(s == 3)
     def _():
         remote(values, vbuf.at[2], d_send, d_recv, sib).wait_recv()
-        last(1, 3, EARLY)
+
+        def body(k, c, wide):
+            take(k, c, 1)
+            use(k, c, wide, 1, 3)
+
+        each(0, EARLY, lambda k, c, wide: use(k, c, wide, 1, 3))
+        each(EARLY, CHUNKS, body)
+        relay(0, slice(None), 1).wait_send()
 
     @pl.when(first)
     def _():

time: 53.9 us -> 52.5 us (0.974)
  Pallas kernels: 52.4 us -> 51 us
    pallas_call x1, Pallas kernels: 52.4 us -> 51 us  [per_device(): pl.pallas_call(kernel, out_shape=jax.ShapeDtypeStruct((tokens, width), BF...]
where the time goes in v6:
time: 52.5 us; the launch traced here: 52.4 us
  Pallas kernels  51 us (97%)
  local copies, waits for them, and re-layouts  1.32 us (3%)
    pallas_call x1, Pallas kernels, per_device(): pl.pallas_call(kernel, out_shape=jax.ShapeDtypeStruct((tokens, width), BF...  51 us
    unnamed x1, local copies, waits for them, and re-layouts  1.32 us

profile of v6, /device:TPU:17, one launch (start us, length us, event | category | flops | bytes accessed | tf_op | source)
XLA Modules:
  0.0 52.4 jit_solution(4309686344043030998)
XLA Ops:
  0.0 51.0 %shard_map.55 = bf16[128,8192]{1,0:T(8,128)(2,1)S(1)} custom-call(bf16[128,8192]{1,0:T(8,128)(2,1)} %bitcast.5, bf16[128,8192]{1,0:T(8,128)(2,1)} %bitcast.6, bf16[128,128]{1,0:T(8,128)(2,1)} %w_in.1, bf16[1,128]{1,0:T(2,128)(2,1)} %bitcast.7, s32[1,4]{1,0:T(1,128)} %ids.1), custom_call_target="tpu_custom_call" | custom-call | tf_op jit(solution)/shard_map/pallas_call | solution.py:392
  51.0 1.3 %copy.7 = bf16[1,128,8192]{2,1,0:T(8,128)(2,1)} copy(bf16[1,128,8192]{2,1,0:T(8,128)(2,1)S(1)} %bitcast.4) | data formatting | bytes 4194304

commit v7 on v6

--- a/solution.py
+++ b/solution.py
@@ -48,7 +48,7 @@
 def kernel(
     hidden, values, w_in, w_beta, ids, out,
     hid, wbuf, vbuf, kown, kbuf, mats, acc, lacc,
-    wb, idm, ready, go, hid_sem, w_sem, wb_sem, id_sem, y_send, y_recv, x_send, x_recv, ring_send, zr_recv, zl_recv,
+    wb, idm, ready, go, hid_sem, w_sem, wb_sem, id_sem, y_send, y_recv, x_send, x_recv, ring_send, ring_recv,
     s_send, s_recv, k_send, k_recv, v_send, v_recv, r_send, r_recv, d_send, d_recv,
 ):
     s, f = lax.axis_index("seg"), lax.axis_index("fsdp")
@@ -159,19 +159,17 @@
         xs, g = lax.rem(x + X - (0, *X_ORDER)[j], X), min(j, 1)
         if t < half or j < X // 2:
             b = wbuf.at[block(1 - t), xs]
-            remote(b, b, ring_send, zr_recv.at[t - 1, g], right).start()
+            remote(b, b, ring_send, ring_recv.at[t - 1, g], right).start()
         if t < half or j >= X // 2:
             b = wbuf.at[block(t - 1), xs]
-            remote(b, b, ring_send, zl_recv.at[t - 1, g], left).start()
+            remote(b, b, ring_send, ring_recv.at[t - 1, g], left).start()
 
     def came(t, g):
-        for sem, n in (
-            (zr_recv, (1, 3)[g] if t < half else 1),
-            (zl_recv, (1, 3)[g] if t < half else 2 * g),
-        ):
-            if n:
-                b = wbuf.at[0, pl.ds(0, n)]
-                remote(b, b, ring_send, sem.at[t - 1, g], left).wait_recv()
+        if t < half:
+            b = wbuf.at[pl.ds(0, 2), pl.ds(0, (1, 3)[g])]
+        else:
+            b = wbuf.at[0, pl.ds(0, (1, 3)[g])]
+        remote(b, b, ring_send, ring_recv.at[t - 1, g], left).wait_recv()
 
     @pl.when(first)
     def _():
@@ -235,24 +233,25 @@
     turned = pltpu.roll(proj, 64, 1)
     logit = dot_t(jnp.ones((8, 128), F32), lacc[...])
     gate = 1.0 / (1.0 + jnp.exp(-logit))
-    kown[0:64, :] = jnp.where(low_half, turned[0:64], proj[64:128]).astype(BF16)
-    kown[64:80, :] = jnp.concatenate(parts(gate), axis=0)
-
-    def k_copy(src, r, to):
-        return remote(src, kbuf.at[r], k_send, k_recv.at[r], to)
-
+    kown[1, 0:64, :] = jnp.where(low_half, turned[0:64], proj[64:128]).astype(BF16)
+    kown[1, 64:80, :] = jnp.concatenate(parts(gate), axis=0)
+
+    def k_copy(src, lo, n, to):
+        return remote(src, kbuf.at[pl.ds(lo, n)], k_send, k_recv.at[lo // 2], to)
+
+    k_own = kown.at[pl.ds(1, 1)]
     v_sib = remote(values, vbuf.at[s], d_send, d_recv, sib)
 
     @pl.when(first)
     def _():
-        k_copy(kown, s, sib).start()
+        remote(k_own, kbuf.at[pl.ds(s, 1)], k_send, k_recv.at[lax.div(s, 2)], sib).start()
         v_sib.start()
 
     @pl.when(s == 1)
     def _():
-        k_copy(kown, 1, cross).start()
-        k_copy(kown, 0, sib).wait_recv()
-        k_copy(kbuf.at[0], 0, cross).start()
+        k_copy(k_own, 0, 1, sib).wait_recv()
+        kown[0] = kbuf[0]
+        k_copy(kown, 0, 2, cross).start()
         v_start(EARLY, CHUNKS, 1)
 
     phi_q = phi_of(halves(proj, turned, low))
@@ -268,17 +267,17 @@
     pl.when(s == 2)(lambda: each(0, HALFWAY, lambda k, c, _: take(k, c, 0)))
     pl.when(s == 3)(lambda: each(0, EARLY, lambda k, c, _: take(k, c, 1)))
 
+    k_two = kbuf.at[pl.ds(0, 2)]
+
     @pl.when(s == 2)
     def _():
-        for r in (1, 0):
-            k_copy(kown, r, sib).wait_recv()
+        k_copy(k_two, 0, 2, sib).wait_recv()
 
     @pl.when(s == 3)
     def _():
-        for r in (1, 0):
-            k_copy(kown, r, cross).wait_recv()
-            k_copy(kbuf.at[r], r, sib).start()
-        k_copy(kown, 2, sib).wait_recv()
+        k_copy(k_two, 0, 2, cross).wait_recv()
+        k_copy(k_two, 0, 2, sib).start()
+        k_copy(k_own, 2, 1, sib).wait_recv()
 
     @pl.when(s > 0)
     def _():
@@ -363,7 +362,7 @@
 
     @pl.when(first)
     def _():
-        k_copy(kown, s, sib).wait_send()
+        k_copy(k_own, 0, 1, sib).wait_send()
         v_sib.wait_send()
 
     @pl.when(second)
@@ -373,8 +372,7 @@
             remote(b, b, sem, s_recv.at[0], sib).wait_send()
         b = wbuf.at[0, pl.ds(0, X - 1)]
         remote(b, b, x_send, x_recv, sib).wait_send()
-        b = kbuf.at[pl.ds(0, 2)]
-        remote(b, b, k_send, k_recv.at[0], sib).wait_send()
+        k_copy(k_two, 0, 2, sib).wait_send()
 
     @pl.when(s == 3)
     def _():
@@ -398,15 +396,15 @@
             pltpu.VMEM((tokens, width), BF16),
             pltpu.VMEM((Z, X, YL, 144, 128), BF16),
             pltpu.VMEM((SEGS - 1, tokens, width), BF16),
-            pltpu.VMEM((80, 128), BF16),
+            pltpu.VMEM((2, 80, 128), BF16),
             pltpu.VMEM((SEGS - 1, 80, 128), BF16),
             pltpu.VMEM((tokens, 128 * (SEGS - 1)), BF16),
             pltpu.VMEM((tokens, 128), F32),
             pltpu.VMEM((tokens, 128), F32),
             pltpu.VMEM((1, 128), BF16), pltpu.SMEM((1, SEGS), jnp.int32),
             pltpu.SemaphoreType.REGULAR, pltpu.SemaphoreType.REGULAR,
-            dma, dma, dma, dma, dma, dma, dma, dma, dma, dma((Z // 2, 2)), dma((Z // 2, 2)),
-            dma, dma((Z // 2 + 1,)), dma, dma((SEGS - 1,)),
+            dma, dma, dma, dma, dma, dma, dma, dma, dma, dma((Z // 2, 2)),
+            dma, dma((Z // 2 + 1,)), dma, dma((2,)),
             dma, dma((CHUNKS,)), dma, dma((CHUNKS,)), dma, dma,
         ],
         compiler_params=pltpu.CompilerParams(

time: 52.5 us -> 52.4 us (level)
  no operation moved by 1% of the time
where the time goes in v7:
time: 52.4 us; the launch traced here: 52.3 us
  Pallas kernels  50.9 us (97%)
  local copies, waits for them, and re-layouts  1.32 us (3%)
    pallas_call x1, Pallas kernels, per_device(): pl.pallas_call(kernel, out_shape=jax.ShapeDtypeStruct((tokens, width), BF...  50.9 us
    unnamed x1, local copies, waits for them, and re-layouts  1.32 us

profile of v7, /device:TPU:17, one launch (start us, length us, event | category | flops | bytes accessed | tf_op | source)
XLA Modules:
  0.0 52.3 jit_solution(2385992169947174690)
XLA Ops:
  0.0 50.9 %shard_map.55 = bf16[128,8192]{1,0:T(8,128)(2,1)S(1)} custom-call(bf16[128,8192]{1,0:T(8,128)(2,1)} %bitcast.5, bf16[128,8192]{1,0:T(8,128)(2,1)} %bitcast.6, bf16[128,128]{1,0:T(8,128)(2,1)} %w_in.1, bf16[1,128]{1,0:T(2,128)(2,1)} %bitcast.7, s32[1,4]{1,0:T(1,128)} %ids.1), custom_call_target="tpu_custom_call" | custom-call | tf_op jit(solution)/shard_map/pallas_call | solution.py:390
  51.0 1.3 %copy.7 = bf16[1,128,8192]{2,1,0:T(8,128)(2,1)} copy(bf16[1,128,8192]{2,1,0:T(8,128)(2,1)S(1)} %bitcast.4) | data formatting | bytes 4194304

commit v8 on v7

--- a/solution.py
+++ b/solution.py
@@ -184,15 +184,17 @@
 
     @pl.when(second)
     def _():
-        wb_copy.wait()
-        wbuf[z, x, yl, 128:144, :] = jnp.broadcast_to(wb[...], (16, 128))
-        w_copy.wait()
-
         @pl.when(s == 1)
         def _():
             pl.semaphore_wait(barrier, len(near))
             v_start(0, EARLY, 1)
-            pl.semaphore_wait(go, 1)
+
+
+        wb_copy.wait()
+        wbuf[z, x, yl, 128:144, :] = jnp.broadcast_to(wb[...], (16, 128))
+        w_copy.wait()
+
+        pl.when(s == 1)(lambda: pl.semaphore_wait(go, 1))
 
         @pl.when(s == 3)
         def _():

time: 52.4 us -> 52.4 us (level)
  no operation moved by 1% of the time
where the time goes in v8:
time: 52.4 us; the launch traced here: 52.3 us
  Pallas kernels  50.9 us (97%)
  local copies, waits for them, and re-layouts  1.32 us (3%)
    pallas_call x1, Pallas kernels, per_device(): pl.pallas_call(kernel, out_shape=jax.ShapeDtypeStruct((tokens, width), BF...  50.9 us
    unnamed x1, local copies, waits for them, and re-layouts  1.32 us

profile of v8, /device:TPU:17, one launch (start us, length us, event | category | flops | bytes accessed | tf_op | source)
XLA Modules:
  0.0 52.3 jit_solution(5498204420657085744)
XLA Ops:
  0.0 50.9 %shard_map.55 = bf16[128,8192]{1,0:T(8,128)(2,1)S(1)} custom-call(bf16[128,8192]{1,0:T(8,128)(2,1)} %bitcast.5, bf16[128,8192]{1,0:T(8,128)(2,1)} %bitcast.6, bf16[128,128]{1,0:T(8,128)(2,1)} %w_in.1, bf16[1,128]{1,0:T(2,128)(2,1)} %bitcast.7, s32[1,4]{1,0:T(1,128)} %ids.1), custom_call_target="tpu_custom_call" | custom-call | tf_op jit(solution)/shard_map/pallas_call | solution.py:392
  51.0 1.3 %copy.7 = bf16[1,128,8192]{2,1,0:T(8,128)(2,1)} copy(bf16[1,128,8192]{2,1,0:T(8,128)(2,1)S(1)} %bitcast.4) | data formatting | bytes 4194304

commit v9 on v7

--- a/solution.py
+++ b/solution.py
@@ -10,9 +10,9 @@
 NU = 3
 X, Z, YL, SEGS = 4, 8, 2, 4
 X_ORDER = (1, 3, 2)
-GROUPS = ((0, 1, 4096), (1, 8, 512))
-CHUNKS = 9
-EARLY = 2
+GROUPS = ((0, 1, 4608), (1, 7, 512))
+CHUNKS = 8
+EARLY = 1
 HALFWAY = 2
 STEP = 512
 MESH = pl.DeviceIdType.MESH

time: 52.4 us -> 52.4 us (level)
  no operation moved by 1% of the time
where the time goes in v9:
time: 52.4 us; the launch traced here: 52.3 us
  Pallas kernels  50.9 us (97%)
  local copies, waits for them, and re-layouts  1.32 us (3%)
    pallas_call x1, Pallas kernels, per_device(): pl.pallas_call(kernel, out_shape=jax.ShapeDtypeStruct((tokens, width), BF...  50.9 us
    unnamed x1, local copies, waits for them, and re-layouts  1.32 us

profile of v9, /device:TPU:17, one launch (start us, length us, event | category | flops | bytes accessed | tf_op | source)
XLA Modules:
  0.0 52.3 jit_solution(17429311816693297817)
XLA Ops:
  0.0 50.9 %shard_map.55 = bf16[128,8192]{1,0:T(8,128)(2,1)S(1)} custom-call(bf16[128,8192]{1,0:T(8,128)(2,1)} %bitcast.5, bf16[128,8192]{1,0:T(8,128)(2,1)} %bitcast.6, bf16[128,128]{1,0:T(8,128)(2,1)} %w_in.1, bf16[1,128]{1,0:T(2,128)(2,1)} %bitcast.7, s32[1,4]{1,0:T(1,128)} %ids.1), custom_call_target="tpu_custom_call" | custom-call | tf_op jit(solution)/shard_map/pallas_call | solution.py:390
  50.9 1.3 %copy.7 = bf16[1,128,8192]{2,1,0:T(8,128)(2,1)} copy(bf16[1,128,8192]{2,1,0:T(8,128)(2,1)S(1)} %bitcast.4) | data formatting | bytes 4194304
